TPU v7x, 32 devices: a whole 2x2x4 slice. The times are simulated.
32 devices in a mesh: lat: 4 (over y, x), lon: 2 (over core), obs: 4 (over z).
Axes of the slice: x: 2, y: 2, z: 4, core: 2. Of those that a mesh axis runs over, the one named last changes fastest.
Arguments:
- coords: bfloat16 [2048, 2, 256], P(('lat', 'lon', 'obs')), may hold values from 0 to 1
- values: bfloat16 [2048, 8, 256], P(('lat', 'lon', 'obs')), may hold values from -6 to 6
- live: int32 [2048, 256], P(('lat', 'lon', 'obs')), may hold values 0 or 1
- tile_of: int32 [2048, 1], P(('lat', 'lon', 'obs')), may hold values from 0 to 7; in each aligned block of 64 rows (0 to 63, 64 to 127, ...) at most 16 rows name the same one
- lengthscale: float32 [9], replicated, may hold values from 0.7 to 6
- w_in: float32 [9, 256], replicated, may hold values from -0.3 to 0.3
- w_conv: bfloat16 [3, 3, 256, 256], replicated, may hold values from -0.125 to 0.125
- grad_out: bfloat16 [128, 256, 256], P(('lat', 'obs'), 'lon'), may hold values from -6 to 6
Outputs:
- grad_conv: float32 [3, 3, 256, 256], replicated
- grad_in: float32 [9, 256], replicated
- grad_values: float32 [2048, 8, 256], P(('lat', 'lon', 'obs'))
Inputs may be any that keep to these rules, and one draw needn't show every extreme that they name: `tile_of`: in the rows of one device at most 16 blocks name the same tile, a bound that some block reaches. `live`: 1 marks an observation, 0 a padding slot.
All inputs are finite; a program needn't handle non-finite values. No bound on the sum of `live` on one device may be relied on, other than what follows from the above.
Results may differ from a plain program's by a relative error of at most 0.0031.
Values may be sent and summed in bfloat16 or wider, within the bound.
A program may use at most 64 MiB of HBM per device.

v0:
```python
import jax
import jax.numpy as jnp
from jax import lax
from jax.sharding import PartitionSpec as P

blocks_per_step = 8


def with_halo(cells, sides, width):
    for axis, dim in sides:
        count = lax.axis_size(axis)
        head = lax.slice_in_dim(cells, 0, width, axis=dim)
        tail = lax.slice_in_dim(cells, cells.shape[dim] - width, cells.shape[dim], axis=dim)
        cells = jnp.concatenate(
            [
                lax.ppermute(tail, axis, [(i, (i + 1) % count) for i in range(count)]),
                cells,
                lax.ppermute(head, axis, [((i + 1) % count, i) for i in range(count)]),
            ],
            axis=dim,
        )
    return cells


def kernel_rows(positions, count, scales):
    centers = jnp.arange(count, dtype=jnp.float32) + 0.5
    diff = centers[:, None] - positions[..., None, :]
    inverse = 1.0 / (2.0 * scales * scales)
    square = diff * diff
    return jnp.exp(-square[..., None, :, :] * inverse[:, None, None])


def with_rims(field):
    padded = with_halo(field, ((("lat", "obs"), 0), ("lon", 1)), 1)
    place = lax.axis_index("lat") * lax.axis_size("obs") + lax.axis_index("obs")
    last_place = lax.axis_size("lat") * lax.axis_size("obs") - 1
    row_ids = jnp.arange(padded.shape[0])
    keep = jnp.where(
        row_ids == 0, place > 0, jnp.where(row_ids == padded.shape[0] - 1, place < last_place, True)
    )
    return padded * keep[:, None, None].astype(padded.dtype)


def body(coords, values, live, tile_of, lengthscale, w_in, w_conv, grad_out):
    lat_count = lax.axis_size("lat")
    lon_count = lax.axis_size("lon")
    obs_count = lax.axis_size("obs")
    tiles = lat_count * lon_count
    blocks = coords.shape[0]
    width = coords.shape[2]
    variables = values.shape[1]
    capacity = 2 * blocks // tiles
    slots_total = tiles * capacity
    rows_dev, tile_cols, channels = grad_out.shape
    tile_rows = rows_dev * obs_count
    live_mask = live.astype(jnp.bfloat16)
    weighted = jnp.concatenate([values * live_mask[:, None, :], live_mask[:, None, :]], axis=1)
    target = tile_of[:, 0]
    onehot = (target[:, None] == jnp.arange(tiles, dtype=jnp.int32)[None, :]).astype(jnp.int32)
    earlier = jnp.cumsum(onehot, axis=0) - onehot
    slot = target * capacity + jnp.sum(earlier * onehot, axis=1)
    send_coords = jnp.zeros((slots_total, 2, width), jnp.bfloat16).at[slot].set(coords)
    send_weighted = (
        jnp.zeros((slots_total, variables + 1, width), jnp.bfloat16).at[slot].set(weighted)
    )
    got_coords, got_weighted = (
        lax.all_to_all(send_coords, ("lat", "lon"), split_axis=0, concat_axis=0, tiled=True),
        lax.all_to_all(send_weighted, ("lat", "lon"), split_axis=0, concat_axis=0, tiled=True),
    )
    steps_count = slots_total // blocks_per_step

    def pieces(index):
        start = index * blocks_per_step
        piece_c = lax.dynamic_slice_in_dim(got_coords, start, blocks_per_step, 0).astype(
            jnp.float32
        )
        piece_w = lax.dynamic_slice_in_dim(got_weighted, start, blocks_per_step, 0).astype(
            jnp.float32
        )
        row_pos = piece_c[:, 0, :].reshape(-1) * tile_rows
        col_pos = piece_c[:, 1, :].reshape(-1) * tile_cols
        flat_w = piece_w.transpose(1, 0, 2).reshape(variables + 1, -1)
        return (row_pos, col_pos, flat_w)

    def forward_step(index, total):
        row_pos, col_pos, flat_w = pieces(index)
        left = (kernel_rows(row_pos, tile_rows, lengthscale) * flat_w[:, None, :]).astype(
            jnp.bfloat16
        )
        right = kernel_rows(col_pos, tile_cols, lengthscale).astype(jnp.bfloat16)
        return total + jnp.einsum("kin,kjn->kij", left, right, preferred_element_type=jnp.float32)

    partial_value = lax.fori_loop(
        0, steps_count, forward_step, jnp.zeros((variables + 1, tile_rows, tile_cols), jnp.float32)
    )
    whole_grid = lax.psum(partial_value, "obs")
    grid = lax.dynamic_slice_in_dim(whole_grid, lax.axis_index("obs") * rows_dev, rows_dev, 1)
    encoded = jnp.einsum("kij,kc->ijc", grid, w_in, precision=lax.Precision.HIGHEST).astype(
        jnp.bfloat16
    )
    padded = with_rims(encoded)
    pre = jnp.zeros((rows_dev, tile_cols, channels), jnp.float32)
    for p in range(3):
        for q in range(3):
            pre = pre + jnp.einsum(
                "ijc,cd->ijd",
                padded[p : p + rows_dev, q : q + tile_cols],
                w_conv[p, q],
                preferred_element_type=jnp.float32,
            )
    slope = (
        0.5 * (1.0 + lax.erf(pre * 0.7071067811865476))
        + pre * jnp.exp(-0.5 * pre * pre) * 0.3989422804014327
    )
    grad_pre = (grad_out.astype(jnp.float32) * slope).astype(jnp.bfloat16)
    padded_grad = with_rims(grad_pre)
    terms = []
    back = grad_out.astype(jnp.float32)
    for p in range(3):
        for q in range(3):
            terms.append(
                jnp.einsum(
                    "ijc,ijd->cd",
                    padded[p : p + rows_dev, q : q + tile_cols],
                    grad_pre,
                    preferred_element_type=jnp.float32,
                )
            )
            back = back + jnp.einsum(
                "ijd,cd->ijc",
                padded_grad[2 - p : 2 - p + rows_dev, 2 - q : 2 - q + tile_cols],
                w_conv[p, q],
                preferred_element_type=jnp.float32,
            )
    conv_part = jnp.stack(terms).reshape(3, 3, channels, channels)
    input_part = jnp.einsum("kij,ijc->kc", grid, back, precision=lax.Precision.HIGHEST)
    grad_grid = jnp.einsum(
        "ijc,kc->kij", back, w_in[:variables], precision=lax.Precision.HIGHEST
    ).astype(jnp.bfloat16)
    grad_conv, grad_in = lax.psum((conv_part, input_part), ("lat", "lon", "obs"))
    tile_grad = lax.all_gather(grad_grid, "obs", axis=1, tiled=True)

    def backward_step(index, done):
        row_pos, col_pos, flat_w = pieces(index)
        left = kernel_rows(row_pos, tile_rows, lengthscale[:variables])
        right = kernel_rows(col_pos, tile_cols, lengthscale[:variables]).astype(jnp.bfloat16)
        middle = jnp.einsum("kij,kjn->kin", tile_grad, right, preferred_element_type=jnp.float32)
        term = jnp.sum(left * middle, axis=1) * flat_w[variables][None, :]
        term = term.reshape(variables, blocks_per_step, width).transpose(1, 0, 2)
        return lax.dynamic_update_slice_in_dim(done, term, index * blocks_per_step, 0)

    slot_grads = lax.fori_loop(
        0, steps_count, backward_step, jnp.zeros((slots_total, variables, width), jnp.float32)
    )
    returned = lax.all_to_all(slot_grads, ("lat", "lon"), split_axis=0, concat_axis=0, tiled=True)
    grad_values = returned[slot]
    return (grad_conv, grad_in, grad_values)


def solution(mesh):
    placed = (
        P(("lat", "lon", "obs"), None, None),
        P(("lat", "lon", "obs"), None, None),
        P(("lat", "lon", "obs"), None),
        P(("lat", "lon", "obs"), None),
        P(),
        P(),
        P(),
        P(("lat", "obs"), "lon", None),
    )
    return jax.shard_map(
        body,
        mesh=mesh,
        in_specs=placed,
        out_specs=(P(), P(), P(("lat", "lon", "obs"), None, None)),
        check_vma=False,
    )
```

profile of v0, /device:TPU:0, one launch (start us, length us, event | category | flops | bytes accessed | tf_op | source)
XLA Modules:
  0.0 300.8 jit_solution(13745626643698178361)
XLA Ops:
  13.4 7.1 %scatter_fusion.1 = bf16[128,9,256]{2,1,0:T(8,128)(2,1)} fusion(bf16[128,9,256]{2,1,0:T(8,128)(2,1)} %broadcast_in_dim.83, s32[64]{0:T(128)S(1)} %fusion.101, bf16[64,9,256]{2,1,0:T(8,128)(2,1)S(1)} %pad_maximum_fusion), kind=kCustom, calls=%fused_computation.2 | custom fusion | bytes 884992 | tf_op jit(solution)/shard_map/scatter | solution.py:64
  20.5 5.3 %all-to-all-start.1 = ((bf16[128,9,256]{2,1,0:T(8,128)(2,1)}), bf16[128,9,256]{2,1,0:T(8,128)(2,1)S(1)}, u32[]{:S(2)}, u32[]{:S(2)}) async-start(bf16[128,9,256]{2,1,0:T(8,128)(2,1)} %scatter_fusion.1), calls=%async_computation.1 | async-start | bytes 2097152 | tf_op jit(solution)/shard_map/all_to_all | solution.py:68
  26.5 7.7 %scatter_fusion = bf16[128,2,256]{2,1,0:T(2,128)(2,1)} fusion(bf16[128,2,256]{2,1,0:T(2,128)(2,1)} %broadcast_in_dim.82, s32[64]{0:T(128)S(1)} %fusion.101, bf16[64,2,256]{2,1,0:T(2,128)(2,1)S(1)} %copy-done.3), kind=kCustom, calls=%fused_computation.1 | custom fusion | bytes 196864 | tf_op jit(solution)/shard_map/scatter | solution.py:62
  34.3 6.9 %all-to-all-done.1 = bf16[128,9,256]{2,1,0:T(8,128)(2,1)S(1)} async-done(((bf16[128,9,256]{2,1,0:T(8,128)(2,1)}), bf16[128,9,256]{2,1,0:T(8,128)(2,1)S(1)}, u32[]{:S(2)}, u32[]{:S(2)}) %all-to-all-start.1) | async-done | bytes 589856 | tf_op jit(solution)/shard_map/all_to_all | solution.py:68
  41.2 3.4 %all-to-all-start = ((bf16[128,2,256]{2,1,0:T(2,128)(2,1)}), bf16[128,2,256]{2,1,0:T(2,128)(2,1)S(1)}, u32[]{:S(2)}, u32[]{:S(2)}) async-start(bf16[128,2,256]{2,1,0:T(2,128)(2,1)} %scatter_fusion), calls=%async_computation | async-start | bytes 262144 | tf_op jit(solution)/shard_map/all_to_all | solution.py:67
  44.9 5.2 %all-to-all-done = bf16[128,2,256]{2,1,0:T(2,128)(2,1)S(1)} async-done(((bf16[128,2,256]{2,1,0:T(2,128)(2,1)}), bf16[128,2,256]{2,1,0:T(2,128)(2,1)S(1)}, u32[]{:S(2)}, u32[]{:S(2)}) %all-to-all-start) | async-done | bytes 131104 | tf_op jit(solution)/shard_map/all_to_all | solution.py:67
  50.1 39.2 %while.28 = (s32[]{:T(128)}, f32[9,32,128]{2,1,0:T(8,128)S(1)}, bf16[128,2,256]{2,1,0:T(2,128)(2,1)S(1)}, f32[9]{0:T(128)S(1)}, bf16[128,9,256]{2,0,1:T(8,128)(2...) while((s32[]{:T(128)}, f32[9,32,128]{2,1,0:T(8,128)S(1)}, ...), condition=%wide.region_5.6_spmd.clone, body=%wide.region_4.5_spmd.clone.sunk | while | flops 158566592 | bytes 3642909 | solution.py:93
  50.5 1.9 fusion.129
  53.0 1.9 fusion.129
  55.4 1.9 fusion.129
  57.9 1.9 fusion.129
  60.3 1.9 fusion.129
  62.8 1.9 fusion.129
  65.2 1.9 fusion.129
  67.7 1.9 fusion.129
  70.1 1.9 fusion.129
  72.6 1.9 fusion.129
  75.0 1.9 fusion.129
  77.5 1.9 fusion.129
  79.9 1.9 fusion.129
  82.4 1.9 fusion.129
  87.3 1.9 fusion.129
  90.1 34.8 %all-reduce.3.cloned.1.call-done = f32[9,32,128]{2,0,1:T(8,128)} async-done(((f32[9,32,128]{2,0,1:T(8,128)}), f32[9,32,128]{2,0,1:T(8,128)}) %all-reduce.3.cloned.1.call-update) | async-done | bytes 147472 | tf_op jit(solution)/shard_map/psum | solution.py:96
  128.3 4.2 %collective-permute-start.1 = (bf16[1,128,256]{2,1,0:T(8,128)(2,1)S(1)}, bf16[1,128,256]{2,1,0:T(8,128)(2,1)S(1)}, u32[]{:S(2)}, u32[]{:S(2)}) collective-permute-start(bf16[1,128,256]{2,1,0:T(8,128)(2,1)S(1)} %get-tuple-element.287), channel_id=1, source_target_pairs={{1,0},{2,1},{3,2},{8,3},{9,8},{10,9},{11,10},{16,11},{17,16},{18,1... | collective-permute-start | bytes 196616 | tf_op jit(solution)/shard_map/ppermute | solution.py:18
  132.5 2.3 collective-permute-done
  141.0 5.7 %collective-permute-start.5 = (bf16[1,128,256]{2,1,0:T(8,128)(2,1)S(1)}, bf16[1,128,256]{2,1,0:T(8,128)(2,1)S(1)}, u32[]{:S(2)}, u32[]{:S(2)}) collective-permute-start(bf16[1,128,256]{2,1,0:T(8,128)(2,1)S(1)} %get-tuple-element.285), channel_id=1, source_target_pairs={{1,0},{2,1},{3,2},{8,3},{9,8},{10,9},{11,10},{16,11},{17,16},{18,1... | collective-permute-start | bytes 196616 | tf_op jit(solution)/shard_map/ppermute | solution.py:18
  156.2 13.6 %all_gather.3 = bf16[8,32,128]{2,0,1:T(8,128)(2,1)S(1)} all-gather(bf16[8,8,128]{2,0,1:T(8,128)(2,1)S(1)} %fusion.25), channel_id=1, replica_groups=mesh['lat'=4,'lon'=2,'obs'=4] {'obs'}, dimensions={1}, use_global_device_ids=true | all-gather | bytes 81920 | tf_op jit(solution)/shard_map/all_gather | solution.py:141
  170.9 50.2 %while.27 = (s32[]{:T(128)}, f32[128,8,256]{2,1,0:T(8,128)}, bf16[128,2,256]{2,1,0:T(2,128)(2,1)S(1)}, f32[9]{0:T(128)S(1)}, bf16[8,32,128]{2,1,0:T(8,128)(2,1)S...) while((s32[]{:T(128)}, f32[128,8,256]{2,1,0:T(8,128)}, ...), condition=%wide.region_11.12_spmd, body=%wide.region_9.11_spmd.sunk | while | flops 140978368 | bytes 3053055 | solution.py:152
  171.3 2.1 fusion.126
  174.5 2.1 fusion.126
  177.6 2.1 fusion.126
  180.7 2.1 fusion.126
  183.9 2.1 fusion.126
  187.0 2.1 fusion.126
  190.1 2.1 fusion.126
  193.3 2.1 fusion.126
  196.4 2.1 fusion.126
  199.5 2.1 fusion.126
  202.7 2.1 fusion.126
  205.8 2.1 fusion.126
  209.0 2.1 fusion.126
  212.1 2.1 fusion.126
  215.2 2.1 fusion.126
  218.4 2.1 fusion.126
  221.1 3.6 %all-to-all-start.2 = ((f32[128,8,256]{2,1,0:T(8,128)}), f32[128,8,256]{2,1,0:T(8,128)S(1)}, u32[]{:S(2)}, u32[]{:S(2)}) async-start(f32[128,8,256]{2,1,0:T(8,128)} %get-tuple-element.207), calls=%async_computation.2 | async-start | bytes 2097152 | tf_op jit(solution)/shard_map/all_to_all | solution.py:155
  226.1 48.1 %psum.23 = f32[9,256]{1,0:T(8,128)} all-reduce(f32[9,256]{1,0:T(8,128)S(1)} %convolution_bitcast_fusion.9), channel_id=1, replica_groups=mesh['lat'=4,'lon'=2,'obs'=4] {'lat','lon','obs'}, use_global_device_ids=true, to_apply=%region_8.9 | all-reduce | flops 2304 | bytes 18432 | tf_op jit(solution)/shard_map/psum | solution.py:140
  275.6 15.1 %all-reduce.5.cloned.1.call-done = f32[3,3,256,256]{3,2,1,0:T(8,128)} async-done(((f32[3,3,256,256]{3,2,1,0:T(8,128)}), f32[3,3,256,256]{3,2,1,0:T(8,128)}) %all-reduce.5.cloned.1.call-update) | async-done | bytes 2359312 | tf_op jit(solution)/shard_map/psum | solution.py:140
  290.7 3.2 %copy.88 = f32[3,3,256,256]{3,2,1,0:T(8,128)} copy(f32[3,3,256,256]{3,2,1,0:T(8,128)} %all-reduce.5.cloned.1.call-done) | data formatting | bytes 4718592
  (406 shorter events, 55.0 us)
Async XLA Ops:
  20.5 6.0 %copy-start.3 = (bf16[64,2,256]{2,1,0:T(2,128)(2,1)S(1)}, bf16[64,2,256]{2,1,0:T(2,128)(2,1)}, u32[]{:S(2)}) copy-start(bf16[64,2,256]{2,1,0:T(2,128)(2,1)} %param.12) | copy-start | bytes 196612
  20.5 20.7 %all-to-all-start.1 = ((bf16[128,9,256]{2,1,0:T(8,128)(2,1)}), bf16[128,9,256]{2,1,0:T(8,128)(2,1)S(1)}, u32[]{:S(2)}, u32[]{:S(2)}) async-start(bf16[128,9,256]{2,1,0:T(8,128)(2,1)} %scatter_fusion.1), calls=%async_computation.1 | async-start | bytes 2097152 | tf_op jit(solution)/shard_map/all_to_all | solution.py:68
  25.8 24.3 %copy-start.5 = (f32[9]{0:T(128)S(1)}, f32[9]{0:T(128)}, u32[]{:S(2)}) copy-start(f32[9]{0:T(128)} %param.16) | copy-start | bytes 112
  41.2 8.8 %all-to-all-start = ((bf16[128,2,256]{2,1,0:T(2,128)(2,1)}), bf16[128,2,256]{2,1,0:T(2,128)(2,1)S(1)}, u32[]{:S(2)}, u32[]{:S(2)}) async-start(bf16[128,2,256]{2,1,0:T(2,128)(2,1)} %scatter_fusion), calls=%async_computation | async-start | bytes 262144 | tf_op jit(solution)/shard_map/all_to_all | solution.py:67
  44.6 80.3 %all-reduce.3.cloned.1.call-start = ((), (), s32[]{:S(2)}) async-start(), calls=%async_computation.3 | async-start | bytes 524288 | tf_op jit(solution)/shard_map/psum | solution.py:96
  50.1 74.8 %copy-start.4 = (f32[9,256]{1,0:T(8,128)S(1)}, f32[9,256]{1,0:T(8,128)}, u32[]{:S(2)}) copy-start(f32[9,256]{1,0:T(8,128)} %param.17) | copy-start | bytes 27652
  90.1 200.7 %all-reduce.5.cloned.1.call-start = ((), (), s32[]{:S(2)}) async-start(), calls=%async_computation.4 | async-start | bytes 4718592 | tf_op jit(solution)/shard_map/psum | solution.py:140
  90.1 46.5 %copy-start = (bf16[3,3,256,256]{3,2,1,0:T(8,128)(2,1)S(1)}, bf16[3,3,256,256]{3,2,1,0:T(8,128)(2,1)}, u32[]{:S(2)}) copy-start(bf16[3,3,256,256]{3,2,1,0:T(8,128)(2,1)} %param.18) | copy-start | bytes 3538948
  126.8 8.0 %collective-permute-start = (bf16[1,128,256]{2,1,0:T(8,128)(2,1)S(1)}, bf16[1,128,256]{2,1,0:T(8,128)(2,1)S(1)}, u32[]{:S(2)}, u32[]{:S(2)}) collective-permute-start(bf16[1,128,256]{2,1,0:T(8,128)(2,1)S(1)} %get-tuple-element.286), channel_id=1, source_target_pairs={{0,1},{1,2},{2,3},{3,8},{8,9},{9,10},{10,11},{11,16},{16,17},{17,1... | collective-permute-start | bytes 196616 | tf_op jit(solution)/shard_map/ppermute | solution.py:16
  128.3 6.5 %collective-permute-start.1 = (bf16[1,128,256]{2,1,0:T(8,128)(2,1)S(1)}, bf16[1,128,256]{2,1,0:T(8,128)(2,1)S(1)}, u32[]{:S(2)}, u32[]{:S(2)}) collective-permute-start(bf16[1,128,256]{2,1,0:T(8,128)(2,1)S(1)} %get-tuple-element.287), channel_id=1, source_target_pairs={{1,0},{2,1},{3,2},{8,3},{9,8},{10,9},{11,10},{16,11},{17,16},{18,1... | collective-permute-start | bytes 196616 | tf_op jit(solution)/shard_map/ppermute | solution.py:18
  134.8 1.2 collective-permute-start.2
  134.9 1.3 collective-permute-start.3
  138.8 1.0 copy-start.2
  140.9 8.3 %collective-permute-start.4 = (bf16[1,128,256]{2,1,0:T(8,128)(2,1)S(1)}, bf16[1,128,256]{2,1,0:T(8,128)(2,1)S(1)}, u32[]{:S(2)}, u32[]{:S(2)}) collective-permute-start(bf16[1,128,256]{2,1,0:T(8,128)(2,1)S(1)} %get-tuple-element.284), channel_id=1, source_target_pairs={{0,1},{1,2},{2,3},{3,8},{8,9},{9,10},{10,11},{11,16},{16,17},{17,1... | collective-permute-start | bytes 196616 | tf_op jit(solution)/shard_map/ppermute | solution.py:16
  141.0 8.3 %collective-permute-start.5 = (bf16[1,128,256]{2,1,0:T(8,128)(2,1)S(1)}, bf16[1,128,256]{2,1,0:T(8,128)(2,1)S(1)}, u32[]{:S(2)}, u32[]{:S(2)}) collective-permute-start(bf16[1,128,256]{2,1,0:T(8,128)(2,1)S(1)} %get-tuple-element.285), channel_id=1, source_target_pairs={{1,0},{2,1},{3,2},{8,3},{9,8},{10,9},{11,10},{16,11},{17,16},{18,1... | collective-permute-start | bytes 196616 | tf_op jit(solution)/shard_map/ppermute | solution.py:18
  149.3 2.4 collective-permute-start.6
  149.4 2.2 collective-permute-start.7
  150.2 1.4 copy-start.1
  221.1 53.1 %all-to-all-start.2 = ((f32[128,8,256]{2,1,0:T(8,128)}), f32[128,8,256]{2,1,0:T(8,128)S(1)}, u32[]{:S(2)}, u32[]{:S(2)}) async-start(f32[128,8,256]{2,1,0:T(8,128)} %get-tuple-element.207), calls=%async_computation.2 | async-start | bytes 2097152 | tf_op jit(solution)/shard_map/all_to_all | solution.py:155
Sparse Core Ops, SparseCore 0:
  90.2 34.6 all-reduce.2
  151.8 138.9 all-reduce.4
where the time goes:
time: 302 us; the launch traced here: 301 us
  matrix products  78.2 us (26%)
  waiting for transfers between devices  65.2 us (22%)
  blocking collectives  61.8 us (20%)
  other arithmetic  27.3 us (9%)
  local copies, waits for them, and re-layouts  26.6 us (9%)
  starting transfers between devices  24.9 us (8%)
  between operations  14.4 us (5%)
    psum x1, blocking collectives, body(): lax.psum((conv_part, input_part), ('lat', 'lon', 'obs'))  48.1 us
    psum x1, waiting for transfers between devices, body(): whole_grid = lax.psum(partial_value, 'obs')  34.8 us
    dot_general x16, matrix products, backward_step(): jnp.einsum('kij,kjn->kin', tile_grad, right, preferred_element_type=jnp.f...  33.4 us
    dot_general x16, matrix products, forward_step(): jnp.einsum('kin,kjn->kij', left, right, preferred_element_type=jnp.float32)  31.2 us
    psum x1, waiting for transfers between devices, body(): lax.psum((conv_part, input_part), ('lat', 'lon', 'obs'))  15.1 us
    all_gather x1, blocking collectives, body(): tile_grad = lax.all_gather(grad_grid, 'obs', axis=1, tiled=True)  13.6 us
    ppermute x4, starting transfers between devices, with_halo(): lax.ppermute(head, axis, [((i + 1) % count, i) for i in range(count)])  10.9 us
    dynamic_update_slice x16, other arithmetic, backward_step(): lax.dynamic_update_slice_in_dim(done, term, index * blocks_per_step, 0)  10.3 us
  transfers between devices with their start and end apart: 13, of which 7 were waited for; matrix products, arithmetic and copies ran while one was open for 23% of the time, Pallas kernels for 0%

commit v1 on v0

v1 whole, which is shorter than its diff:
```python
import jax
import jax.numpy as jnp
from jax import lax
from jax.experimental import pallas as pl
from jax.experimental.pallas import tpu as pltpu
from jax.sharding import PartitionSpec as P


def with_halo(cells, sides, width):
    for axis, dim in sides:
        count = lax.axis_size(axis)
        head = lax.slice_in_dim(cells, 0, width, axis=dim)
        tail = lax.slice_in_dim(cells, cells.shape[dim] - width, cells.shape[dim], axis=dim)
        cells = jnp.concatenate(
            [
                lax.ppermute(tail, axis, [(i, (i + 1) % count) for i in range(count)]),
                cells,
                lax.ppermute(head, axis, [((i + 1) % count, i) for i in range(count)]),
            ],
            axis=dim,
        )
    return cells


def squares(position, count):
    width = position.shape[1]
    centers = lax.broadcasted_iota(jnp.int32, (count, width), 0).astype(jnp.float32) + 0.5
    diff = centers - position
    return diff * diff


def rates(lengthscale):
    return -1.4426950408889634 / (2.0 * lengthscale * lengthscale)


def gather_kernel(tile_ref, rate_ref, coords_ref, values_ref, live_ref, out_ref, total):
    variables = values_ref.shape[1]
    tile_rows, tile_cols = total.shape[2:]
    rows_dev = out_ref.shape[2]
    total[...] = jnp.zeros_like(total)

    def one(n, carry):
        t = tile_ref[n]
        place = coords_ref[n].astype(jnp.float32)
        mask = live_ref[pl.ds(n, 1), :].astype(jnp.float32)
        weighted = values_ref[n].astype(jnp.float32) * mask
        row_sq = squares(place[0:1] * tile_rows, tile_rows)
        col_sq = squares(place[1:2] * tile_cols, tile_cols)
        for k in range(variables + 1):
            w = weighted[k : k + 1] if k < variables else mask
            left = (jnp.exp2(row_sq * rate_ref[k]) * w).astype(jnp.bfloat16)
            right = jnp.exp2(col_sq * rate_ref[k]).astype(jnp.bfloat16)
            total[t, k] += lax.dot_general(
                left, right, (((1,), (1,)), ((), ())), preferred_element_type=jnp.float32
            )
        return carry

    lax.fori_loop(0, coords_ref.shape[0], one, 0)

    def flush(t, carry):
        for o in range(tile_rows // rows_dev):
            for k in range(variables + 1):
                out_ref[t * (tile_rows // rows_dev) + o, k] = total[
                    t, k, o * rows_dev : (o + 1) * rows_dev
                ].astype(jnp.bfloat16)
        return carry

    lax.fori_loop(0, total.shape[0], flush, 0)


def value_kernel(tile_ref, rate_ref, coords_ref, live_ref, grad_ref, out_ref):
    variables = out_ref.shape[1]
    tile_rows, tile_cols = grad_ref.shape[2:]

    def one(n, carry):
        t = tile_ref[n]
        place = coords_ref[n].astype(jnp.float32)
        mask = live_ref[pl.ds(n, 1), :].astype(jnp.float32)
        row_sq = squares(place[0:1] * tile_rows, tile_rows)
        col_sq = squares(place[1:2] * tile_cols, tile_cols)
        for k in range(variables):
            left = jnp.exp2(row_sq * rate_ref[k])
            right = jnp.exp2(col_sq * rate_ref[k]).astype(jnp.bfloat16)
            middle = jnp.dot(grad_ref[t, k], right, preferred_element_type=jnp.float32)
            out_ref[n, k : k + 1] = jnp.sum(left * middle, axis=0, keepdims=True) * mask
        return carry

    lax.fori_loop(0, coords_ref.shape[0], one, 0)


def with_rims(field):
    padded = with_halo(field, ((("lat", "obs"), 0), ("lon", 1)), 1)
    place = lax.axis_index("lat") * lax.axis_size("obs") + lax.axis_index("obs")
    last_place = lax.axis_size("lat") * lax.axis_size("obs") - 1
    row_ids = jnp.arange(padded.shape[0])
    keep = jnp.where(
        row_ids == 0, place > 0, jnp.where(row_ids == padded.shape[0] - 1, place < last_place, True)
    )
    return padded * keep[:, None, None].astype(padded.dtype)


def body(coords, values, live, tile_of, lengthscale, w_in, w_conv, grad_out):
    lat_count = lax.axis_size("lat")
    lon_count = lax.axis_size("lon")
    obs_count = lax.axis_size("obs")
    tiles = lat_count * lon_count
    blocks = coords.shape[0]
    width = coords.shape[2]
    variables = values.shape[1]
    rows_dev, tile_cols, channels = grad_out.shape
    tile_rows = rows_dev * obs_count
    everyone = ("lat", "lon", "obs")
    rate = rates(lengthscale)
    target = tile_of[:, 0]
    smem = pl.BlockSpec(memory_space=pltpu.SMEM)
    vmem = pl.BlockSpec(memory_space=pltpu.VMEM)
    exps = blocks * width * (tile_rows + tile_cols)
    partial_value = pl.pallas_call(
        gather_kernel,
        out_shape=jax.ShapeDtypeStruct(
            (tiles * obs_count, variables + 1, rows_dev, tile_cols), jnp.bfloat16
        ),
        in_specs=[smem, smem, vmem, vmem, vmem],
        out_specs=vmem,
        scratch_shapes=[
            pltpu.VMEM((tiles, variables + 1, tile_rows, tile_cols), jnp.float32)
        ],
        compiler_params=pltpu.CompilerParams(vmem_limit_bytes=40 * 1024 * 1024),
    )(target, rate, coords, values, live)
    parts = lax.all_to_all(partial_value, everyone, split_axis=0, concat_axis=0, tiled=True)
    grid = jnp.sum(parts.astype(jnp.float32), axis=0)
    encoded = jnp.einsum("kij,kc->ijc", grid, w_in, precision=lax.Precision.HIGHEST).astype(
        jnp.bfloat16
    )
    padded = with_rims(encoded)
    pre = jnp.zeros((rows_dev, tile_cols, channels), jnp.float32)
    for p in range(3):
        for q in range(3):
            pre = pre + jnp.einsum(
                "ijc,cd->ijd",
                padded[p : p + rows_dev, q : q + tile_cols],
                w_conv[p, q],
                preferred_element_type=jnp.float32,
            )
    slope = (
        0.5 * (1.0 + lax.erf(pre * 0.7071067811865476))
        + pre * jnp.exp(-0.5 * pre * pre) * 0.3989422804014327
    )
    grad_pre = (grad_out.astype(jnp.float32) * slope).astype(jnp.bfloat16)
    padded_grad = with_rims(grad_pre)
    terms = []
    back = grad_out.astype(jnp.float32)
    for p in range(3):
        for q in range(3):
            terms.append(
                jnp.einsum(
                    "ijc,ijd->cd",
                    padded[p : p + rows_dev, q : q + tile_cols],
                    grad_pre,
                    preferred_element_type=jnp.float32,
                )
            )
            back = back + jnp.einsum(
                "ijd,cd->ijc",
                padded_grad[2 - p : 2 - p + rows_dev, 2 - q : 2 - q + tile_cols],
                w_conv[p, q],
                preferred_element_type=jnp.float32,
            )
    conv_part = jnp.stack(terms).reshape(3, 3, channels, channels)
    input_part = jnp.einsum("kij,ijc->kc", grid, back, precision=lax.Precision.HIGHEST)
    grad_grid = jnp.einsum(
        "ijc,kc->kij", back, w_in[:variables], precision=lax.Precision.HIGHEST
    ).astype(jnp.bfloat16)
    devices = lat_count * lon_count * obs_count
    pieces = conv_part.reshape(devices, -1, channels).astype(jnp.bfloat16)
    pieces = lax.all_to_all(pieces, everyone, split_axis=0, concat_axis=0, tiled=True)
    piece = jnp.sum(pieces.astype(jnp.float32), axis=0).astype(jnp.bfloat16)
    input_parts = lax.all_gather(input_part, everyone, axis=0, tiled=False)
    grad_in = jnp.sum(input_parts, axis=0)
    tile_grad = lax.all_gather(grad_grid, everyone, axis=0, tiled=False)
    tile_grad = tile_grad.reshape(tiles, obs_count, variables, rows_dev, tile_cols)
    tile_grad = tile_grad.transpose(0, 2, 1, 3, 4).reshape(tiles, variables, tile_rows, tile_cols)
    whole_conv = lax.all_gather(piece, everyone, axis=0, tiled=True)
    grad_conv = whole_conv.astype(jnp.float32).reshape(3, 3, channels, channels)
    grad_values = pl.pallas_call(
        value_kernel,
        out_shape=jax.ShapeDtypeStruct((blocks, variables, width), jnp.float32),
        in_specs=[smem, smem, vmem, vmem, vmem],
        out_specs=vmem,
        compiler_params=pltpu.CompilerParams(vmem_limit_bytes=40 * 1024 * 1024),
        cost_estimate=pl.CostEstimate(
            flops=40000000000, bytes_accessed=4000000, transcendentals=exps * variables
        ),
    )(target, rate, coords, live, tile_grad)
    return (grad_conv, grad_in, grad_values)


def solution(mesh):
    placed = (
        P(("lat", "lon", "obs"), None, None),
        P(("lat", "lon", "obs"), None, None),
        P(("lat", "lon", "obs"), None),
        P(("lat", "lon", "obs"), None),
        P(),
        P(),
        P(),
        P(("lat", "obs"), "lon", None),
    )
    return jax.shard_map(
        body,
        mesh=mesh,
        in_specs=placed,
        out_specs=(P(), P(), P(("lat", "lon", "obs"), None, None)),
        check_vma=False,
    )
```

time: 302 us -> 314 us (1.040)
  blocking collectives: 61.8 us -> 177 us
  matrix products: 78.2 us -> 12 us
  Pallas kernels: 0 us -> 44.8 us
  waiting for transfers between devices: 65.2 us -> 34.8 us
  local copies, waits for them, and re-layouts: 26.6 us -> 5.41 us
  other arithmetic: 27.3 us -> 7.37 us
  starting transfers between devices: 24.9 us -> 18.2 us
    all_gather x1 -> x2, blocking collectives: 13.6 us -> 154 us  [the longest x1 85.8 us: body(): tile_grad = lax.all_gather(grad_grid, everyone, axis=0, tiled=False)]
    dot_general x32 -> x0, matrix products: 64.6 us -> none  [the longest x16 33.4 us: backward_step(): jnp.einsum('kij,kjn->kin', tile_grad, right, preferred_element_type=jnp.f...]
    psum x2 -> x0, waiting for transfers between devices: 49.8 us -> none  [the longest x1 34.8 us: body(): whole_grid = lax.psum(partial_value, 'obs')]
    psum x1 -> x0, blocking collectives: 48.1 us -> none  [body(): lax.psum((conv_part, input_part), ('lat', 'lon', 'obs'))]
    pallas_call x0 -> x2, Pallas kernels: none -> 44.8 us  [the longest x1 23.2 us: body(): pl.pallas_call(gather_kernel, out_shape=jax.ShapeDtypeStruct((tiles * obs...]
    all_gather x0 -> x1, waiting for transfers between devices: none -> 30.9 us  [body(): whole_conv = lax.all_gather(piece, everyone, axis=0, tiled=True)]
    all_to_all x0 -> x1, blocking collectives: none -> 22.7 us  [body(): lax.all_to_all(partial_value, everyone, split_axis=0, concat_axis=0, tile...]
    scatter x2 -> x0, local copies, waits for them, and re-layouts: 14.9 us -> none  [the longest x1 7.74 us: body(): jnp.zeros((slots_total, 2, width), jnp.bfloat16).at[slot].set(coords)]
  transfers between devices with their start and end apart: 13 -> 10, of which waited for: 7 -> 6; matrix products, arithmetic and copies ran while one was open for 23% -> 3% of each run, Pallas kernels for 0% -> 7%
where the time goes in v1:
time: 314 us
  blocking collectives  177 us (56%)
  Pallas kernels  44.8 us (14%)
  waiting for transfers between devices  34.8 us (11%)
  starting transfers between devices  18.2 us (6%)
  between operations  14.4 us (5%)
  matrix products  12 us (4%)
  other arithmetic  7.37 us (2%)
  local copies, waits for them, and re-layouts  5.41 us (2%)
    all_gather x1, blocking collectives, body(): tile_grad = lax.all_gather(grad_grid, everyone, axis=0, tiled=False)  85.8 us
    all_gather x1, blocking collectives, body(): input_parts = lax.all_gather(input_part, everyone, axis=0, tiled=False)  68.2 us
    all_gather x1, waiting for transfers between devices, body(): whole_conv = lax.all_gather(piece, everyone, axis=0, tiled=True)  30.9 us
    pallas_call x1, Pallas kernels, body(): pl.pallas_call(gather_kernel, out_shape=jax.ShapeDtypeStruct((tiles * obs...  23.2 us
    all_to_all x1, blocking collectives, body(): lax.all_to_all(partial_value, everyone, split_axis=0, concat_axis=0, tile...  22.7 us
    pallas_call x1, Pallas kernels, body(): pl.pallas_call(value_kernel, out_shape=jax.ShapeDtypeStruct((blocks, vari...  21.6 us
    ppermute x4, starting transfers between devices, with_halo(): lax.ppermute(head, axis, [((i + 1) % count, i) for i in range(count)])  9.27 us
  transfers between devices with their start and end apart: 10, of which 6 were waited for; matrix products, arithmetic and copies ran while one was open for 3% of the time, Pallas kernels for 7%

profile of v1, /device:TPU:0, one launch (start us, length us, event | category | flops | bytes accessed | tf_op | source)
XLA Modules:
  0.0 313.7 jit_solution(6582345782769756975)
XLA Ops:
  7.2 0.7 fusion.102.rate_ref
  7.8 1.0 copy-done
  8.8 0.8 copy-done.1
  9.6 0.8 copy-done.3
  10.5 0.7 copy-done.5
  11.1 23.2 %shard_map.103 = bf16[32,9,8,128]{3,2,1,0:T(8,128)(2,1)S(1)} custom-call(s32[64]{0:T(128)S(1)} %bitcast.204, f32[9]{0:T(128)S(1)} %fusion.102.rate_ref, bf16[64,2,256]{2,1,0:T(2,128)(2,1)S(1)} %copy-done.1, bf16[64,8,256]{2,1,0:T(8,128)(2,1)S(1)} %copy-done, s32[64,256]{1,0:T(8,128)S(1)} %copy-done.3), custom_call_target="tpu_custom_call" | custom-call | tf_op jit(solution)/shard_map/pallas_call | solution.py:118
  34.4 22.7 %all_to_all.10 = bf16[32,9,8,128]{3,2,1,0:T(8,128)(2,1)S(1)} all-to-all(bf16[32,9,8,128]{3,2,1,0:T(8,128)(2,1)S(1)} %shard_map.103), channel_id=1, replica_groups=mesh['lat'=4,'lon'=2,'obs'=4] {'lat','lon','obs'}, dimensions={0} | all-to-all | bytes 1179648 | tf_op jit(solution)/shard_map/all_to_all | solution.py:130
  57.2 1.0 convolution_convert_fusion
  58.3 2.7 collective-permute-start
  61.0 2.9 collective-permute-start.1
  64.0 2.6 collective-permute-done
  66.7 0.4 collective-permute-start.2
  67.3 0.7 collective-permute-done.2
  68.0 0.3 collective-permute-done.3
  68.3 0.4 maximum_multiply_fusion
  71.3 0.7 copy-done.9
  72.0 0.7 fusion.28
  72.7 0.3 fusion.26
  73.1 5.7 %collective-permute-start.5 = (bf16[1,128,256]{2,1,0:T(8,128)(2,1)S(1)}, bf16[1,128,256]{2,1,0:T(8,128)(2,1)S(1)}, u32[]{:S(2)}, u32[]{:S(2)}) collective-permute-start(bf16[1,128,256]{2,1,0:T(8,128)(2,1)S(1)} %get-tuple-element.8), channel_id=1, source_target_pairs={{1,0},{2,1},{3,2},{8,3},{9,8},{10,9},{11,10},{16,11},{17,16},{18,1... | collective-permute-start | bytes 196616 | tf_op jit(solution)/shard_map/ppermute | solution.py:18
  78.8 0.3 fusion.24
  79.1 0.3 fusion.22
  79.5 0.3 fusion.20
  79.8 0.3 fusion.18
  80.2 0.4 fusion.16
  80.5 0.3 fusion.14
  80.9 0.3 fusion.12
  81.4 0.6 pad_maximum_fusion.2
  82.0 0.5 collective-permute-start.7
  82.5 0.3 fusion.10
  82.9 1.0 copy-done.8
  83.9 5.7 %all-to-all-start.1 = ((bf16[32,72,256]{2,1,0:T(8,128)(2,1)}), bf16[32,72,256]{2,1,0:T(8,128)(2,1)S(1)}, u32[]{:S(2)}, u32[]{:S(2)}) async-start(bf16[32,72,256]{2,1,0:T(8,128)(2,1)} %bitcast.208), calls=%async_computation.1 | async-start | bytes 2359296 | tf_op jit(solution)/shard_map/all_to_all | solution.py:176
  89.7 1.2 maximum_multiply_fusion.1
  90.9 0.3 convolution_add_fusion.8
  91.3 0.4 convolution_add_fusion.7
  92.0 0.4 convolution_add_fusion.5
  92.4 0.4 convolution_add_fusion.4
  93.1 0.3 convolution_add_fusion.2
  93.4 0.4 convolution_add_fusion.1
  94.1 1.0 fusion.27
  95.1 85.8 %all-gather.1 = bf16[256,8,128]{2,0,1:T(8,128)(2,1)S(1)} all-gather(bf16[8,8,128]{2,0,1:T(8,128)(2,1)S(1)} %fusion.27), channel_id=3, replica_groups=mesh['lat'=4,'lon'=2,'obs'=4] {'lat','lon','obs'}, dimensions={0}, use_global_device_ids=true | all-gather | bytes 540672 | tf_op jit(solution)/shard_map/all_gather | solution.py:180
  180.9 0.3 copy.47
  181.2 0.5 convolution_bitcast_fusion.9
  181.8 68.2 %all-gather.2 = f32[32,9,256]{2,1,0:T(8,128)S(1)} all-gather(f32[1,9,256]{2,1,0:T(8,128)S(1)} %convolution_bitcast_fusion.9), channel_id=2, replica_groups=mesh['lat'=4,'lon'=2,'obs'=4] {'lat','lon','obs'}, dimensions={0}, use_global_device_ids=true | all-gather | bytes 304128 | tf_op jit(solution)/shard_map/all_gather | solution.py:178
  250.0 0.7 reduce_sum.32
  250.7 0.8 reduce_sum.31
  251.5 21.6 %shard_map.104 = f32[64,8,256]{2,1,0:T(8,128)} custom-call(s32[64]{0:T(128)S(1)} %bitcast.205, f32[9]{0:T(128)S(1)} %fusion.102.rate_ref, bf16[64,2,256]{2,1,0:T(2,128)(2,1)S(1)} %copy-done.2, s32[64,256]{1,0:T(8,128)S(1)} %copy-done.4, bf16[8,8,32,128]{3,2,1,0:T(8,128)(2,1)S(1)} %bitcast.203), custom_call_target="tpu_custom_call" | custom-call | flops 40000000000 | bytes 4000000 | tf_op jit(solution)/shard_map/pallas_call | solution.py:185
  273.1 30.9 %all-gather.5.cloned.1.call-done = bf16[2304,256]{1,0:T(8,128)(2,1)} async-done(((bf16[72,256]{1,0:T(8,128)(2,1)}), bf16[2304,256]{1,0:T(8,128)(2,1)}) %all-gather.5.cloned.1.call-update) | async-done | bytes 1179664 | tf_op jit(solution)/shard_map/all_gather | solution.py:183
  303.9 2.9 convert.47
  (47 shorter events, 4.2 us)
Async XLA Ops:
  7.8 1.0 copy-start
  8.8 0.8 copy-start.1
  9.6 0.8 copy-start.3
  10.5 0.7 copy-start.5
  11.1 46.1 %copy-start.11 = (f32[9,256]{1,0:T(8,128)S(1)}, f32[9,256]{1,0:T(8,128)}, u32[]{:S(2)}) copy-start(f32[9,256]{1,0:T(8,128)} %param.13) | copy-start | bytes 27652
  58.3 10.5 %copy-start.7 = (bf16[3,3,256,256]{3,2,1,0:T(8,128)(2,1)S(1)}, bf16[3,3,256,256]{3,2,1,0:T(8,128)(2,1)}, u32[]{:S(2)}) copy-start(bf16[3,3,256,256]{3,2,1,0:T(8,128)(2,1)} %param.14) | copy-start | bytes 3538948
  58.3 8.3 %collective-permute-start = (bf16[1,128,256]{2,1,0:T(8,128)(2,1)S(1)}, bf16[1,128,256]{2,1,0:T(8,128)(2,1)S(1)}, u32[]{:S(2)}, u32[]{:S(2)}) collective-permute-start(bf16[1,128,256]{2,1,0:T(8,128)(2,1)S(1)} %get-tuple-element.9), channel_id=1, source_target_pairs={{0,1},{1,2},{2,3},{3,8},{8,9},{9,10},{10,11},{11,16},{16,17},{17,1... | collective-permute-start | bytes 196616 | tf_op jit(solution)/shard_map/ppermute | solution.py:16
  61.0 5.7 %collective-permute-start.1 = (bf16[1,128,256]{2,1,0:T(8,128)(2,1)S(1)}, bf16[1,128,256]{2,1,0:T(8,128)(2,1)S(1)}, u32[]{:S(2)}, u32[]{:S(2)}) collective-permute-start(bf16[1,128,256]{2,1,0:T(8,128)(2,1)S(1)} %get-tuple-element.10), channel_id=1, source_target_pairs={{1,0},{2,1},{3,2},{8,3},{9,8},{10,9},{11,10},{16,11},{17,16},{18,1... | collective-permute-start | bytes 196616 | tf_op jit(solution)/shard_map/ppermute | solution.py:18
  66.7 1.2 collective-permute-start.2
  67.1 1.2 collective-permute-start.3
  67.3 1.4 copy-start.12
  70.9 1.0 copy-start.9
  73.0 8.4 %collective-permute-start.4 = (bf16[1,128,256]{2,1,0:T(8,128)(2,1)S(1)}, bf16[1,128,256]{2,1,0:T(8,128)(2,1)S(1)}, u32[]{:S(2)}, u32[]{:S(2)}) collective-permute-start(bf16[1,128,256]{2,1,0:T(8,128)(2,1)S(1)} %get-tuple-element.7), channel_id=1, source_target_pairs={{0,1},{1,2},{2,3},{3,8},{8,9},{9,10},{10,11},{11,16},{16,17},{17,1... | collective-permute-start | bytes 196616 | tf_op jit(solution)/shard_map/ppermute | solution.py:16
  73.1 8.3 %collective-permute-start.5 = (bf16[1,128,256]{2,1,0:T(8,128)(2,1)S(1)}, bf16[1,128,256]{2,1,0:T(8,128)(2,1)S(1)}, u32[]{:S(2)}, u32[]{:S(2)}) collective-permute-start(bf16[1,128,256]{2,1,0:T(8,128)(2,1)S(1)} %get-tuple-element.8), channel_id=1, source_target_pairs={{1,0},{2,1},{3,2},{8,3},{9,8},{10,9},{11,10},{16,11},{17,16},{18,1... | collective-permute-start | bytes 196616 | tf_op jit(solution)/shard_map/ppermute | solution.py:18
  81.4 1.5 copy-start.10
  82.0 7.7 %collective-permute-start.6 = (bf16[10,1,256]{2,1,0:T(2,128)(2,1)}, bf16[10,1,256]{2,1,0:T(2,128)(2,1)S(1)}, u32[]{:S(2)}, u32[]{:S(2)}) collective-permute-start(bf16[10,1,256]{2,1,0:T(2,128)(2,1)} %get-tuple-element.3), channel_id=1, source_target_pairs={{0,4},{4,0},{1,5},{5,1},{2,6},{6,2},{3,7},{7,3},{8,12},{12,8},{9,1... | collective-permute-start | bytes 15368 | tf_op jit(solution)/shard_map/ppermute | solution.py:16
  82.0 7.7 %collective-permute-start.7 = (bf16[10,1,256]{2,1,0:T(2,128)(2,1)}, bf16[10,1,256]{2,1,0:T(2,128)(2,1)S(1)}, u32[]{:S(2)}, u32[]{:S(2)}) collective-permute-start(bf16[10,1,256]{2,1,0:T(2,128)(2,1)} %get-tuple-element.4), channel_id=1, source_target_pairs={{4,0},{0,4},{5,1},{1,5},{6,2},{2,6},{7,3},{3,7},{12,8},{8,12},{13,... | collective-permute-start | bytes 15368 | tf_op jit(solution)/shard_map/ppermute | solution.py:18
  82.9 1.0 copy-start.8
  83.9 166.7 %all-to-all-start.1 = ((bf16[32,72,256]{2,1,0:T(8,128)(2,1)}), bf16[32,72,256]{2,1,0:T(8,128)(2,1)S(1)}, u32[]{:S(2)}, u32[]{:S(2)}) async-start(bf16[32,72,256]{2,1,0:T(8,128)(2,1)} %bitcast.208), calls=%async_computation.1 | async-start | bytes 2359296 | tf_op jit(solution)/shard_map/all_to_all | solution.py:176
  89.6 214.3 %all-gather.5.cloned.1.call-start = ((), (), s32[]{:S(2)}) async-start(), calls=%async_computation.2 | async-start | bytes 1216512 | tf_op jit(solution)/shard_map/all_gather | solution.py:183
  181.7 69.7 %copy-start.2 = (bf16[64,2,256]{2,1,0:T(2,128)(2,1)S(1)}, bf16[64,2,256]{2,1,0:T(2,128)(2,1)}, u32[]{:S(2)}) copy-start(bf16[64,2,256]{2,1,0:T(2,128)(2,1)} %coords_ref.3) | copy-start | bytes 196612
  181.8 69.7 %copy-start.4 = (s32[64,256]{1,0:T(8,128)S(1)}, s32[64,256]{1,0:T(8,128)}, u32[]{:S(2)}) copy-start(s32[64,256]{1,0:T(8,128)} %live_ref.3) | copy-start | bytes 196612
  181.8 69.7 %copy-start.6 = (s32[64,1]{0,1:T(1,128)S(1)}, s32[64,1]{0,1:T(1,128)}, u32[]{:S(2)}) copy-start(s32[64,1]{0,1:T(1,128)} %param.11) | copy-start | bytes 772
Sparse Core Ops, SparseCore 0:
  251.6 52.3 all-gather.4

commit v2 on v1

--- a/solution.py
+++ b/solution.py
@@ -68,12 +68,128 @@
     lax.fori_loop(0, total.shape[0], flush, 0)
 
 
-def value_kernel(tile_ref, rate_ref, coords_ref, live_ref, grad_ref, out_ref):
-    variables = out_ref.shape[1]
-    tile_rows, tile_cols = grad_ref.shape[2:]
+def signal_peers(axes):
+    barrier = pltpu.get_barrier_semaphore()
+    greeted = 0
+    for axis in axes:
+        count = lax.axis_size(axis)
+        me = lax.axis_index(axis)
+        for step in range(1, count):
+            pl.semaphore_signal(
+                barrier,
+                inc=1,
+                device_id={axis: lax.rem(me + step, count)},
+                device_id_type=pl.DeviceIdType.MESH,
+            )
+            greeted += 1
+    pl.semaphore_wait(barrier, greeted)
+
+
+def start_copies(axis, source_of, target, sems):
+    count = lax.axis_size(axis)
+    me = lax.axis_index(axis)
+    copies = []
+    for step in range(1, count):
+        peer = lax.rem(me + step, count)
+        copy = pltpu.make_async_remote_copy(
+            src_ref=source_of(peer),
+            dst_ref=target,
+            send_sem=sems.at[0, step],
+            recv_sem=sems.at[1, step],
+            device_id={axis: peer},
+            device_id_type=pl.DeviceIdType.MESH,
+        )
+        copy.start()
+        copies.append(copy)
+    return copies
+
+
+def wait_all(copies):
+    for copy in copies:
+        copy.wait()
+
+
+def value_kernel(
+    slot_ref,
+    rate_ref,
+    coords_ref,
+    live_ref,
+    grad_ref,
+    input_ref,
+    conv_ref,
+    out_ref,
+    input_out,
+    conv_out,
+    cells,
+    tile_grad,
+    own_in1,
+    own_in2,
+    in1,
+    in2,
+    in3,
+    got1,
+    sum1,
+    got2,
+    sum2,
+    got3,
+    whole,
+    sems,
+):
+    blocks, variables = out_ref.shape[:2]
+    lat_count, lon_count, obs_count = (lax.axis_size(a) for a in ("lat", "lon", "obs"))
+    lat, lon, obs = (lax.axis_index(a) for a in ("lat", "lon", "obs"))
+    tile_rows, tile_cols = tile_grad.shape[2:]
+    rows_dev = tile_rows // obs_count
+    signal_peers(("lat", "lon", "obs"))
+
+    reduce1 = start_copies("lon", lambda peer: conv_ref.at[peer], got1.at[lon], sems.at[0])
+    home = lon * lat_count + lat
+    cells[home, obs] = grad_ref[...]
+    in1[obs] = input_ref[...]
+    mine = cells.at[home, obs]
+    gather1 = start_copies("obs", lambda peer: mine, mine, sems.at[1])
+    gather1 += start_copies("obs", lambda peer: input_ref, in1.at[obs], sems.at[2])
+    wait_all(gather1)
+    total = jnp.sum(in1[...], axis=0)
+    own_in1[...] = total
+    in2[lat] = total
+    gather2 = start_copies("lat", lambda peer: cells.at[home], cells.at[home], sems.at[3])
+    gather2 += start_copies("lat", lambda peer: own_in1, in2.at[lat], sems.at[4])
+
+    wait_all(reduce1)
+
+    def add1(i, carry):
+        value = conv_ref[lon, i]
+        for step in range(1, lon_count):
+            value = value + got1[lax.rem(lon + step, lon_count), i]
+        sum1[i // obs_count, i % obs_count] = value.astype(jnp.bfloat16)
+        return carry
+
+    lax.fori_loop(0, lat_count * obs_count, add1, 0)
+    reduce2 = start_copies("lat", lambda peer: sum1.at[peer], got2.at[lat], sems.at[5])
+    wait_all(gather2)
+    total = jnp.sum(in2[...], axis=0)
+    own_in2[...] = total
+    in3[lon] = total
+    group = pl.ds(lon * lat_count, lat_count)
+    gather3 = start_copies("lon", lambda peer: cells.at[group], cells.at[group], sems.at[6])
+    gather3 += start_copies("lon", lambda peer: own_in2, in3.at[lon], sems.at[7])
+    wait_all(gather3)
+    input_out[...] = jnp.sum(in3[...], axis=0)
+
+    def spread(t, carry):
+        for o in range(obs_count):
+            piece = cells[t, o].astype(jnp.float32)
+            for k in range(variables):
+                tile_grad[t, k, o * rows_dev : (o + 1) * rows_dev] = piece[
+                    k * rows_dev : (k + 1) * rows_dev
+                ]
+        return carry
+
+    lax.fori_loop(0, tile_grad.shape[0], spread, 0)
 
     def one(n, carry):
-        t = tile_ref[n]
+        t = slot_ref[n]
         place = coords_ref[n].astype(jnp.float32)
         mask = live_ref[pl.ds(n, 1), :].astype(jnp.float32)
         row_sq = squares(place[0:1] * tile_rows, tile_rows)
@@ -81,11 +197,53 @@
         for k in range(variables):
             left = jnp.exp2(row_sq * rate_ref[k])
             right = jnp.exp2(col_sq * rate_ref[k]).astype(jnp.bfloat16)
-            middle = jnp.dot(grad_ref[t, k], right, preferred_element_type=jnp.float32)
+            middle = jnp.dot(
+                tile_grad[t, k].astype(jnp.bfloat16), right, preferred_element_type=jnp.float32
+            )
             out_ref[n, k : k + 1] = jnp.sum(left * middle, axis=0, keepdims=True) * mask
         return carry
 
-    lax.fori_loop(0, coords_ref.shape[0], one, 0)
+    def some(first, last):
+        lax.fori_loop(first * blocks // 64, last * blocks // 64, one, 0)
+
+    some(0, 8)
+    wait_all(reduce2)
+
+    def add2(i, carry):
+        value = sum1[lat, i].astype(jnp.float32)
+        for step in range(1, lat_count):
+            value = value + got2[lax.rem(lat + step, lat_count), i].astype(jnp.float32)
+        sum2[i] = value
+        return carry
+
+    lax.fori_loop(0, obs_count, add2, 0)
+    reduce3 = start_copies("obs", lambda peer: sum2.at[peer], got3.at[obs], sems.at[8])
+    some(8, 24)
+    wait_all(reduce3)
+    value = sum2[obs]
+    for step in range(1, obs_count):
+        value = value + got3[lax.rem(obs + step, obs_count)]
+    whole[lon, lat, obs] = value.astype(jnp.bfloat16)
+    mine1 = whole.at[lon, lat, obs]
+    spread1 = start_copies("obs", lambda peer: mine1, mine1, sems.at[9])
+    some(24, 34)
+    wait_all(spread1)
+    mine2 = whole.at[lon, lat]
+    spread2 = start_copies("lat", lambda peer: mine2, mine2, sems.at[10])
+    some(34, 54)
+    wait_all(spread2)
+    mine3 = whole.at[lon]
+    spread3 = start_copies("lon", lambda peer: mine3, mine3, sems.at[11])
+    some(54, 64)
+    wait_all(spread3)
+
+    def give(i, carry):
+        a, b = i // lat_count, i % lat_count
+        for o in range(obs_count):
+            conv_out[a, b, o] = whole[a, b, o]
+        return carry
+
+    lax.fori_loop(0, lon_count * lat_count, give, 0)
 
 
 def with_rims(field):
@@ -171,27 +329,54 @@
     grad_grid = jnp.einsum(
         "ijc,kc->kij", back, w_in[:variables], precision=lax.Precision.HIGHEST
     ).astype(jnp.bfloat16)
-    devices = lat_count * lon_count * obs_count
-    pieces = conv_part.reshape(devices, -1, channels).astype(jnp.bfloat16)
-    pieces = lax.all_to_all(pieces, everyone, split_axis=0, concat_axis=0, tiled=True)
-    piece = jnp.sum(pieces.astype(jnp.float32), axis=0).astype(jnp.bfloat16)
-    input_parts = lax.all_gather(input_part, everyone, axis=0, tiled=False)
-    grad_in = jnp.sum(input_parts, axis=0)
-    tile_grad = lax.all_gather(grad_grid, everyone, axis=0, tiled=False)
-    tile_grad = tile_grad.reshape(tiles, obs_count, variables, rows_dev, tile_cols)
-    tile_grad = tile_grad.transpose(0, 2, 1, 3, 4).reshape(tiles, variables, tile_rows, tile_cols)
-    whole_conv = lax.all_gather(piece, everyone, axis=0, tiled=True)
-    grad_conv = whole_conv.astype(jnp.float32).reshape(3, 3, channels, channels)
-    grad_values = pl.pallas_call(
+    chunk = conv_part.size // (lat_count * lon_count * obs_count * channels)
+    most = max(lat_count, lon_count, obs_count)
+    held = ((variables + 1 + 7) // 8) * 8
+    input_part = jnp.pad(input_part, ((0, held - variables - 1), (0, 0)))
+    f32, bf16 = jnp.float32, jnp.bfloat16
+    slots = (target % lon_count) * lat_count + target // lon_count
+    grad_values, grad_in, whole_conv = pl.pallas_call(
         value_kernel,
-        out_shape=jax.ShapeDtypeStruct((blocks, variables, width), jnp.float32),
-        in_specs=[smem, smem, vmem, vmem, vmem],
-        out_specs=vmem,
-        compiler_params=pltpu.CompilerParams(vmem_limit_bytes=40 * 1024 * 1024),
+        out_shape=(
+            jax.ShapeDtypeStruct((blocks, variables, width), f32),
+            jax.ShapeDtypeStruct((held, channels), f32),
+            jax.ShapeDtypeStruct((lon_count, lat_count, obs_count, chunk, channels), bf16),
+        ),
+        in_specs=[smem, smem, vmem, vmem, vmem, vmem, vmem],
+        out_specs=(vmem, vmem, vmem),
+        scratch_shapes=[
+            pltpu.VMEM((tiles, obs_count, variables * rows_dev, tile_cols), bf16),
+            pltpu.VMEM((tiles, variables, tile_rows, tile_cols), f32),
+            pltpu.VMEM((held, channels), f32),
+            pltpu.VMEM((held, channels), f32),
+            pltpu.VMEM((obs_count, held, channels), f32),
+            pltpu.VMEM((lat_count, held, channels), f32),
+            pltpu.VMEM((lon_count, held, channels), f32),
+            pltpu.VMEM((lon_count, lat_count * obs_count, chunk, channels), f32),
+            pltpu.VMEM((lat_count, obs_count, chunk, channels), bf16),
+            pltpu.VMEM((lat_count, obs_count, chunk, channels), bf16),
+            pltpu.VMEM((obs_count, chunk, channels), f32),
+            pltpu.VMEM((obs_count, chunk, channels), f32),
+            pltpu.VMEM((lon_count, lat_count, obs_count, chunk, channels), bf16),
+            pltpu.SemaphoreType.DMA((12, 2, most)),
+        ],
+        compiler_params=pltpu.CompilerParams(
+            vmem_limit_bytes=48 * 1024 * 1024, collective_id=1, has_side_effects=True
+        ),
         cost_estimate=pl.CostEstimate(
-            flops=40000000000, bytes_accessed=4000000, transcendentals=exps * variables
+            flops=4000000000, bytes_accessed=8000000, transcendentals=exps * variables
         ),
-    )(target, rate, coords, live, tile_grad)
+    )(
+        slots,
+        rate,
+        coords,
+        live,
+        grad_grid.reshape(variables * rows_dev, tile_cols),
+        input_part,
+        conv_part.reshape(lon_count, lat_count * obs_count, chunk, channels),
+    )
+    grad_in = grad_in[: variables + 1]
+    grad_conv = whole_conv.astype(f32).reshape(3, 3, channels, channels)
     return (grad_conv, grad_in, grad_values)
 
 

time: 314 us -> 130 us (0.41)
  blocking collectives: 177 us -> 22.7 us
  waiting for transfers between devices: 34.8 us -> 4.19 us
  Pallas kernels: 44.8 us -> 68.2 us
  between operations: 14.4 us -> 0.99 us
  starting transfers between devices: 18.2 us -> 12.7 us
  other arithmetic: 7.37 us -> 3.23 us
    all_gather x2 -> x0, blocking collectives: 154 us -> none  [the longest x1 85.8 us: body(): tile_grad = lax.all_gather(grad_grid, everyone, axis=0, tiled=False)]
    all_gather x1 -> x0, waiting for transfers between devices: 30.9 us -> none  [body(): whole_conv = lax.all_gather(piece, everyone, axis=0, tiled=True)]
    pallas_call x1, Pallas kernels: 21.6 us -> 45 us  [body(): pl.pallas_call(value_kernel, out_shape=(jax.ShapeDtypeStruct((blocks, var...]
    all_to_all x1 -> x0, starting transfers between devices: 5.7 us -> none  [body(): lax.all_to_all(pieces, everyone, split_axis=0, concat_axis=0, tiled=True)]
  transfers between devices with their start and end apart: 10 -> 8, of which waited for: 6 -> 6; matrix products, arithmetic and copies ran while one was open for 3% -> 2% of each run, Pallas kernels for 7% -> 0%
where the time goes in v2:
time: 130 us; the launch traced here: 129 us
  Pallas kernels  68.2 us (52%)
  blocking collectives  22.7 us (17%)
  starting transfers between devices  12.7 us (10%)
  matrix products  11.9 us (9%)
  local copies, waits for them, and re-layouts  5.47 us (4%)
  waiting for transfers between devices  4.19 us (3%)
  other arithmetic  3.23 us (2%)
    pallas_call x1, Pallas kernels, body(): pl.pallas_call(value_kernel, out_shape=(jax.ShapeDtypeStruct((blocks, var...  45 us
    pallas_call x1, Pallas kernels, body(): pl.pallas_call(gather_kernel, out_shape=jax.ShapeDtypeStruct((tiles * obs...  23.2 us
    all_to_all x1, blocking collectives, body(): lax.all_to_all(partial_value, everyone, split_axis=0, concat_axis=0, tile...  22.7 us
    ppermute x4, starting transfers between devices, with_halo(): lax.ppermute(head, axis, [((i + 1) % count, i) for i in range(count)])  9.43 us
    unnamed x20, local copies, waits for them, and re-layouts  5.42 us
    ppermute x4, waiting for transfers between devices, with_halo(): lax.ppermute(tail, axis, [(i, (i + 1) % count) for i in range(count)])  3.6 us
    ppermute x4, starting transfers between devices, with_halo(): lax.ppermute(tail, axis, [(i, (i + 1) % count) for i in range(count)])  3.31 us
    dot_general x9, matrix products, body(): jnp.einsum('ijc,cd->ijd', padded[p:p + rows_dev, q:q + tile_cols], w_conv...  3.15 us
  transfers between devices with their start and end apart: 8, of which 6 were waited for; matrix products, arithmetic and copies ran while one was open for 2% of the time, Pallas kernels for 0%

profile of v2, /device:TPU:0, one launch (start us, length us, event | category | flops | bytes accessed | tf_op | source)
XLA Modules:
  0.0 129.5 jit_solution(13777878838195825155)
XLA Ops:
  0.6 0.7 fusion.84.rate_ref
  1.3 1.0 copy-done
  2.2 0.8 copy-done.1
  3.1 0.8 copy-done.3
  3.9 0.7 copy-done.5
  4.6 23.2 %shard_map.103 = bf16[32,9,8,128]{3,2,1,0:T(8,128)(2,1)S(1)} custom-call(s32[64]{0:T(128)S(1)} %bitcast.141, f32[9]{0:T(128)S(1)} %fusion.84.rate_ref, bf16[64,2,256]{2,1,0:T(2,128)(2,1)S(1)} %copy-done.1, bf16[64,8,256]{2,1,0:T(8,128)(2,1)S(1)} %copy-done, s32[64,256]{1,0:T(8,128)S(1)} %copy-done.3), custom_call_target="tpu_custom_call" | custom-call | tf_op jit(solution)/shard_map/pallas_call | solution.py:276
  27.8 22.7 %all_to_all.5 = bf16[32,9,8,128]{3,2,1,0:T(8,128)(2,1)S(1)} all-to-all(bf16[32,9,8,128]{3,2,1,0:T(8,128)(2,1)S(1)} %shard_map.103), channel_id=1, replica_groups=mesh['lat'=4,'lon'=2,'obs'=4] {'lat','lon','obs'}, dimensions={0} | all-to-all | bytes 1179648 | tf_op jit(solution)/shard_map/all_to_all | solution.py:288
  50.7 1.0 convolution_convert_fusion
  51.8 2.7 %collective-permute-start = (bf16[1,128,256]{2,1,0:T(8,128)(2,1)S(1)}, bf16[1,128,256]{2,1,0:T(8,128)(2,1)S(1)}, u32[]{:S(2)}, u32[]{:S(2)}) collective-permute-start(bf16[1,128,256]{2,1,0:T(8,128)(2,1)S(1)} %get-tuple-element.15), channel_id=1, source_target_pairs={{0,1},{1,2},{2,3},{3,8},{8,9},{9,10},{10,11},{11,16},{16,17},{17,1... | collective-permute-start | bytes 196616 | tf_op jit(solution)/shard_map/ppermute | solution.py:16
  54.5 3.0 %collective-permute-start.1 = (bf16[1,128,256]{2,1,0:T(8,128)(2,1)S(1)}, bf16[1,128,256]{2,1,0:T(8,128)(2,1)S(1)}, u32[]{:S(2)}, u32[]{:S(2)}) collective-permute-start(bf16[1,128,256]{2,1,0:T(8,128)(2,1)S(1)} %get-tuple-element.16), channel_id=1, source_target_pairs={{1,0},{2,1},{3,2},{8,3},{9,8},{10,9},{11,10},{16,11},{17,16},{18,1... | collective-permute-start | bytes 196616 | tf_op jit(solution)/shard_map/ppermute | solution.py:18
  57.4 2.6 %collective-permute-done = bf16[1,128,256]{2,1,0:T(8,128)(2,1)S(1)} collective-permute-done((bf16[1,128,256]{2,1,0:T(8,128)(2,1)S(1)}, bf16[1,128,256]{2,1,0:T(8,128)(2,1)S(1)}, u32[]{:S(2)}, u32[]{:S(2)}) %collective-permute-start) | collective-permute-done | bytes 65568 | tf_op jit(solution)/shard_map/ppermute | solution.py:16
  60.2 0.4 collective-permute-start.2
  60.8 0.7 collective-permute-done.2
  61.4 0.3 collective-permute-done.3
  61.8 0.4 maximum_multiply_fusion
  62.8 0.3 convolution_add_fusion.15
  63.4 0.3 convolution_add_fusion.13
  63.7 0.3 convolution_add_fusion.12
  64.4 0.3 convolution_add_fusion.10
  64.7 0.7 copy-done.7
  65.4 0.7 fusion.10
  66.1 0.3 fusion.8
  66.5 5.9 %collective-permute-start.5 = (bf16[1,128,256]{2,1,0:T(8,128)(2,1)S(1)}, bf16[1,128,256]{2,1,0:T(8,128)(2,1)S(1)}, u32[]{:S(2)}, u32[]{:S(2)}) collective-permute-start(bf16[1,128,256]{2,1,0:T(8,128)(2,1)S(1)} %get-tuple-element.14), channel_id=1, source_target_pairs={{1,0},{2,1},{3,2},{8,3},{9,8},{10,9},{11,10},{16,11},{17,16},{18,1... | collective-permute-start | bytes 196616 | tf_op jit(solution)/shard_map/ppermute | solution.py:18
  72.4 0.3 fusion.7
  72.7 0.4 fusion.6
  73.1 0.3 fusion.5
  73.5 0.4 fusion.4
  73.8 0.3 fusion.3
  74.2 0.3 fusion.2
  74.5 0.4 fusion.1
  75.0 0.5 collective-permute-start.7
  75.5 0.3 fusion
  76.3 0.4 maximum_multiply_fusion.1
  76.7 0.3 convolution_add_fusion.8
  77.1 0.3 convolution_add_fusion.7
  77.5 0.3 convolution_add_fusion.6
  77.8 0.4 convolution_add_fusion.5
  78.1 0.4 convolution_add_fusion.4
  78.5 0.3 convolution_add_fusion.3
  78.8 0.3 convolution_add_fusion.2
  79.2 0.4 convolution_add_fusion.1
  79.6 0.3 convolution_add_fusion
  79.9 0.5 convolution_bitcast_fusion.9
  80.4 1.0 fusion.9
  81.5 45.0 %shard_map.104 = (f32[64,8,256]{2,1,0:T(8,128)S(1)}, f32[16,256]{1,0:T(8,128)S(1)}, bf16[2,4,4,72,256]{4,3,2,1,0:T(8,128)(2,1)S(1)}) custom-call(s32[64]{0:T(128)S(1)} %fusion.86.slot_ref, f32[9]{0:T(128)S(1)} %fusion.84.rate_ref, bf16[64,2,256]{2,1,0:T(2,128)(2,1)S(1)} %copy-done.2, s32[64,256]{1,0:T(8,128)S(1)} %copy-done.4, ...), custom_call_target="tpu_custom_call" | custom-call | flops 4000000000 | bytes 8000000 | tf_op jit(solution)/shard_map/pallas_call | solution.py:338
  126.5 1.6 %convert.1 = f32[3,3,256,256]{3,2,1,0:T(8,128)} convert(bf16[3,3,256,256]{3,2,1,0:T(8,128)(2,1)S(1)} %bitcast.138) | non-fusion elementwise | flops 589824 | bytes 3538944 | tf_op jit(solution)/shard_map/reshape | solution.py:379
  128.1 0.6 copy.58
  128.7 0.8 copy.59
  (34 shorter events, 2.3 us)
Async XLA Ops:
  1.3 1.0 copy-start
  2.2 0.8 copy-start.1
  3.1 0.8 copy-start.3
  3.9 0.7 copy-start.5
  4.6 46.1 %copy-start.8 = (f32[9,256]{1,0:T(8,128)S(1)}, f32[9,256]{1,0:T(8,128)}, u32[]{:S(2)}) copy-start(f32[9,256]{1,0:T(8,128)} %param.13) | copy-start | bytes 27652
  50.7 11.5 %copy-start.6 = (bf16[3,3,256,256]{3,2,1,0:T(8,128)(2,1)S(1)}, bf16[3,3,256,256]{3,2,1,0:T(8,128)(2,1)}, u32[]{:S(2)}) copy-start(bf16[3,3,256,256]{3,2,1,0:T(8,128)(2,1)} %param.14) | copy-start | bytes 3538948
  51.8 8.3 %collective-permute-start = (bf16[1,128,256]{2,1,0:T(8,128)(2,1)S(1)}, bf16[1,128,256]{2,1,0:T(8,128)(2,1)S(1)}, u32[]{:S(2)}, u32[]{:S(2)}) collective-permute-start(bf16[1,128,256]{2,1,0:T(8,128)(2,1)S(1)} %get-tuple-element.15), channel_id=1, source_target_pairs={{0,1},{1,2},{2,3},{3,8},{8,9},{9,10},{10,11},{11,16},{16,17},{17,1... | collective-permute-start | bytes 196616 | tf_op jit(solution)/shard_map/ppermute | solution.py:16
  54.5 5.7 %collective-permute-start.1 = (bf16[1,128,256]{2,1,0:T(8,128)(2,1)S(1)}, bf16[1,128,256]{2,1,0:T(8,128)(2,1)S(1)}, u32[]{:S(2)}, u32[]{:S(2)}) collective-permute-start(bf16[1,128,256]{2,1,0:T(8,128)(2,1)S(1)} %get-tuple-element.16), channel_id=1, source_target_pairs={{1,0},{2,1},{3,2},{8,3},{9,8},{10,9},{11,10},{16,11},{17,16},{18,1... | collective-permute-start | bytes 196616 | tf_op jit(solution)/shard_map/ppermute | solution.py:18
  60.2 1.3 collective-permute-start.2
  60.6 1.2 collective-permute-start.3
  64.4 1.0 copy-start.7
  66.5 8.4 %collective-permute-start.4 = (bf16[1,128,256]{2,1,0:T(8,128)(2,1)S(1)}, bf16[1,128,256]{2,1,0:T(8,128)(2,1)S(1)}, u32[]{:S(2)}, u32[]{:S(2)}) collective-permute-start(bf16[1,128,256]{2,1,0:T(8,128)(2,1)S(1)} %get-tuple-element.13), channel_id=1, source_target_pairs={{0,1},{1,2},{2,3},{3,8},{8,9},{9,10},{10,11},{11,16},{16,17},{17,1... | collective-permute-start | bytes 196616 | tf_op jit(solution)/shard_map/ppermute | solution.py:16
  66.5 8.4 %collective-permute-start.5 = (bf16[1,128,256]{2,1,0:T(8,128)(2,1)S(1)}, bf16[1,128,256]{2,1,0:T(8,128)(2,1)S(1)}, u32[]{:S(2)}, u32[]{:S(2)}) collective-permute-start(bf16[1,128,256]{2,1,0:T(8,128)(2,1)S(1)} %get-tuple-element.14), channel_id=1, source_target_pairs={{1,0},{2,1},{3,2},{8,3},{9,8},{10,9},{11,10},{16,11},{17,16},{18,1... | collective-permute-start | bytes 196616 | tf_op jit(solution)/shard_map/ppermute | solution.py:18
  74.9 1.2 collective-permute-start.6
  75.0 1.3 %collective-permute-start.7 = (bf16[10,1,256]{2,1,0:T(2,128)(2,1)S(1)}, bf16[10,1,256]{2,1,0:T(2,128)(2,1)S(1)}, u32[]{:S(2)}, u32[]{:S(2)}) collective-permute-start(bf16[10,1,256]{2,1,0:T(2,128)(2,1)S(1)} %get-tuple-element.10), channel_id=1, source_target_pairs={{4,0},{0,4},{5,1},{1,5},{6,2},{2,6},{7,3},{3,7},{12,8},{8,12},{13,... | collective-permute-start | bytes 15368 | tf_op jit(solution)/shard_map/ppermute | solution.py:18
  79.9 1.6 %copy-start.2 = (bf16[64,2,256]{2,1,0:T(2,128)(2,1)S(1)}, bf16[64,2,256]{2,1,0:T(2,128)(2,1)}, u32[]{:S(2)}) copy-start(bf16[64,2,256]{2,1,0:T(2,128)(2,1)} %coords_ref.3) | copy-start | bytes 196612
  79.9 1.6 %copy-start.4 = (s32[64,256]{1,0:T(8,128)S(1)}, s32[64,256]{1,0:T(8,128)}, u32[]{:S(2)}) copy-start(s32[64,256]{1,0:T(8,128)} %live_ref.3) | copy-start | bytes 196612

commit v3 on v2

--- a/solution.py
+++ b/solution.py
@@ -36,7 +36,7 @@
 def gather_kernel(tile_ref, rate_ref, coords_ref, values_ref, live_ref, out_ref, total):
     variables = values_ref.shape[1]
     tile_rows, tile_cols = total.shape[2:]
-    rows_dev = out_ref.shape[2]
+    rows_dev = out_ref.shape[3]
     total[...] = jnp.zeros_like(total)
 
     def one(n, carry):
@@ -60,17 +60,14 @@
     def flush(t, carry):
         for o in range(tile_rows // rows_dev):
             for k in range(variables + 1):
-                out_ref[t * (tile_rows // rows_dev) + o, k] = total[
-                    t, k, o * rows_dev : (o + 1) * rows_dev
-                ].astype(jnp.bfloat16)
+                out_ref[t, o, k] = total[t, k, o * rows_dev : (o + 1) * rows_dev]
         return carry
 
     lax.fori_loop(0, total.shape[0], flush, 0)
 
 
-def signal_peers(axes):
+def signal_peers(axes, greeted=0):
     barrier = pltpu.get_barrier_semaphore()
-    greeted = 0
     for axis in axes:
         count = lax.axis_size(axis)
         me = lax.axis_index(axis)
@@ -107,6 +104,80 @@
 def wait_all(copies):
     for copy in copies:
         copy.wait()
+
+
+def reduce_kernel(part_ref, out_ref, got1, sum1, got2, sum2, got3, rows, sides, sems):
+    lat_count, lon_count, obs_count = (lax.axis_size(a) for a in ("lat", "lon", "obs"))
+    lat, lon, obs = (lax.axis_index(a) for a in ("lat", "lon", "obs"))
+    rows_dev = rows.shape[0] - 2
+    levels = sum1.shape[2] // rows_dev
+    mesh_ids = pl.DeviceIdType.MESH
+    places = lat_count * obs_count
+    place = lat * obs_count + obs
+    after = lax.rem(place + 1, places)
+    before = lax.rem(place + places - 1, places)
+    down = {"lat": after // obs_count, "obs": lax.rem(after, obs_count)}
+    up = {"lat": before // obs_count, "obs": lax.rem(before, obs_count)}
+    east = {"lon": lax.rem(lon + 1, lon_count)}
+    west = {"lon": lax.rem(lon + lon_count - 1, lon_count)}
+    rows[...] = jnp.zeros_like(rows)
+    barrier = pltpu.get_barrier_semaphore()
+    for device in (up, down):
+        pl.semaphore_signal(barrier, inc=1, device_id=device, device_id_type=mesh_ids)
+    signal_peers(("lat", "lon", "obs"), 2)
+
+    wait_all(start_copies("lon", lambda peer: part_ref.at[peer], got1.at[lon], sems.at[0]))
+
+    def add1(i, carry):
+        value = part_ref[lon, i]
+        for step in range(1, lon_count):
+            value = value + got1[lax.rem(lon + step, lon_count), i]
+        sum1[i // obs_count, i % obs_count] = value.astype(jnp.bfloat16)
+        return carry
+
+    lax.fori_loop(0, lat_count * obs_count, add1, 0)
+    wait_all(start_copies("lat", lambda peer: sum1.at[peer], got2.at[lat], sems.at[1]))
+
+    def add2(i, carry):
+        value = sum1[lat, i].astype(jnp.float32)
+        for step in range(1, lat_count):
+            value = value + got2[lax.rem(lat + step, lat_count), i].astype(jnp.float32)
+        sum2[i] = value
+        return carry
+
+    lax.fori_loop(0, obs_count, add2, 0)
+    wait_all(start_copies("obs", lambda peer: sum2.at[peer], got3.at[obs], sems.at[2]))
+    value = sum2[obs]
+    for step in range(1, obs_count):
+        value = value + got3[lax.rem(obs + step, obs_count)]
+    for k in range(levels):
+        for r in range(rows_dev):
+            rows[r + 1, k : k + 1] = value[k * rows_dev + r : k * rows_dev + r + 1]
+
+    def send(source, target, number, device):
+        copy = pltpu.make_async_remote_copy(
+            src_ref=source,
+            dst_ref=target,
+            send_sem=sems.at[3, 0, number],
+            recv_sem=sems.at[3, 1, number],
+            device_id=device,
+            device_id_type=mesh_ids,
+        )
+        copy.start()
+        return copy
+
+    wait_all(
+        [
+            send(rows.at[1], rows.at[rows_dev + 1], 0, up),
+            send(rows.at[rows_dev], rows.at[0], 1, down),
+        ]
+    )
+    rows[0] = rows[0] * (place > 0).astype(jnp.float32)
+    rows[rows_dev + 1] = rows[rows_dev + 1] * (place < places - 1).astype(jnp.float32)
+    wait_all([send(rows, sides.at[1], 2, west), send(rows, sides.at[0], 3, east)])
+    out_ref[0] = sides[0]
+    out_ref[1] = rows[...]
+    out_ref[2] = sides[1]
 
 
 def value_kernel(
@@ -273,24 +344,46 @@
     smem = pl.BlockSpec(memory_space=pltpu.SMEM)
     vmem = pl.BlockSpec(memory_space=pltpu.VMEM)
     exps = blocks * width * (tile_rows + tile_cols)
+    f32, bf16 = jnp.float32, jnp.bfloat16
+    slots = (target % lon_count) * lat_count + target // lon_count
     partial_value = pl.pallas_call(
         gather_kernel,
-        out_shape=jax.ShapeDtypeStruct(
-            (tiles * obs_count, variables + 1, rows_dev, tile_cols), jnp.bfloat16
-        ),
+        out_shape=jax.ShapeDtypeStruct((tiles, obs_count, variables + 1, rows_dev, tile_cols), f32),
         in_specs=[smem, smem, vmem, vmem, vmem],
         out_specs=vmem,
+        scratch_shapes=[pltpu.VMEM((tiles, variables + 1, tile_rows, tile_cols), f32)],
+        compiler_params=pltpu.CompilerParams(vmem_limit_bytes=40 * 1024 * 1024),
+    )(slots, rate, coords, values, live)
+    depth = (variables + 1) * rows_dev
+    held = ((variables + 1 + 7) // 8) * 8
+    most = max(lat_count, lon_count, obs_count, 4)
+    sides = pl.pallas_call(
+        reduce_kernel,
+        out_shape=jax.ShapeDtypeStruct((3, rows_dev + 2, held, tile_cols), f32),
+        in_specs=[vmem],
+        out_specs=vmem,
         scratch_shapes=[
-            pltpu.VMEM((tiles, variables + 1, tile_rows, tile_cols), jnp.float32)
+            pltpu.VMEM((lon_count, lat_count * obs_count, depth, tile_cols), f32),
+            pltpu.VMEM((lat_count, obs_count, depth, tile_cols), bf16),
+            pltpu.VMEM((lat_count, obs_count, depth, tile_cols), bf16),
+            pltpu.VMEM((obs_count, depth, tile_cols), f32),
+            pltpu.VMEM((obs_count, depth, tile_cols), f32),
+            pltpu.VMEM((rows_dev + 2, held, tile_cols), f32),
+            pltpu.VMEM((2, rows_dev + 2, held, tile_cols), f32),
+            pltpu.SemaphoreType.DMA((4, 2, most)),
         ],
-        compiler_params=pltpu.CompilerParams(vmem_limit_bytes=40 * 1024 * 1024),
-    )(target, rate, coords, values, live)
-    parts = lax.all_to_all(partial_value, everyone, split_axis=0, concat_axis=0, tiled=True)
-    grid = jnp.sum(parts.astype(jnp.float32), axis=0)
-    encoded = jnp.einsum("kij,kc->ijc", grid, w_in, precision=lax.Precision.HIGHEST).astype(
+        compiler_params=pltpu.CompilerParams(
+            vmem_limit_bytes=40 * 1024 * 1024, collective_id=2, has_side_effects=True
+        ),
+    )(partial_value.reshape(lon_count, lat_count * obs_count, depth, tile_cols))
+    level = variables + 1
+    wide = jnp.concatenate(
+        [sides[0, :, :level, -1:], sides[1, :, :level], sides[2, :, :level, :1]], axis=2
+    )
+    grid = sides[1, 1 : rows_dev + 1, :level].transpose(1, 0, 2)
+    padded = jnp.einsum("ikj,kc->ijc", wide, w_in, precision=lax.Precision.HIGHEST).astype(
         jnp.bfloat16
     )
-    padded = with_rims(encoded)
     pre = jnp.zeros((rows_dev, tile_cols, channels), jnp.float32)
     for p in range(3):
         for q in range(3):
@@ -330,11 +423,7 @@
         "ijc,kc->kij", back, w_in[:variables], precision=lax.Precision.HIGHEST
     ).astype(jnp.bfloat16)
     chunk = conv_part.size // (lat_count * lon_count * obs_count * channels)
-    most = max(lat_count, lon_count, obs_count)
-    held = ((variables + 1 + 7) // 8) * 8
     input_part = jnp.pad(input_part, ((0, held - variables - 1), (0, 0)))
-    f32, bf16 = jnp.float32, jnp.bfloat16
-    slots = (target % lon_count) * lat_count + target // lon_count
     grad_values, grad_in, whole_conv = pl.pallas_call(
         value_kernel,
         out_shape=(

time: 130 us -> 123 us (0.946)
  Pallas kernels: 68.2 us -> 92.9 us
  blocking collectives: 22.7 us -> 0 us
  starting transfers between devices: 12.7 us -> 6.25 us
  waiting for transfers between devices: 4.19 us -> 0.83 us
    pallas_call x1 -> x2, Pallas kernels: 23.2 us -> 48.9 us  [the longest x1 25.7 us: body(): pl.pallas_call(reduce_kernel, out_shape=jax.ShapeDtypeStruct((3, rows_dev...]
    all_to_all x1 -> x0, blocking collectives: 22.7 us -> none  [body(): lax.all_to_all(partial_value, everyone, split_axis=0, concat_axis=0, tile...]
    ppermute x4 -> x2, starting transfers between devices: 9.43 us -> 6.12 us  [with_halo(): lax.ppermute(head, axis, [((i + 1) % count, i) for i in range(count)])]
    ppermute x4 -> x2, starting transfers between devices: 3.31 us -> 0.13 us  [with_halo(): lax.ppermute(tail, axis, [(i, (i + 1) % count) for i in range(count)])]
    ppermute x4 -> x2, waiting for transfers between devices: 3.6 us -> 0.66 us  [with_halo(): lax.ppermute(tail, axis, [(i, (i + 1) % count) for i in range(count)])]
    unnamed x20 -> x22, local copies, waits for them, and re-layouts: 5.42 us -> 4.78 us
  transfers between devices with their start and end apart: 8 -> 4, of which waited for: 6 -> 2; matrix products, arithmetic and copies ran while one was open for 2% -> 3% of each run, Pallas kernels for 0% -> 0%
where the time goes in v3:
time: 123 us
  Pallas kernels  92.9 us (76%)
  matrix products  12.5 us (10%)
  starting transfers between devices  6.25 us (5%)
  local copies, waits for them, and re-layouts  5.56 us (5%)
  other arithmetic  3.38 us (3%)
    pallas_call x1, Pallas kernels, body(): pl.pallas_call(value_kernel, out_shape=(jax.ShapeDtypeStruct((blocks, var...  44 us
    pallas_call x1, Pallas kernels, body(): pl.pallas_call(reduce_kernel, out_shape=jax.ShapeDtypeStruct((3, rows_dev...  25.7 us
    pallas_call x1, Pallas kernels, body(): pl.pallas_call(gather_kernel, out_shape=jax.ShapeDtypeStruct((tiles, obs_...  23.2 us
    ppermute x2, starting transfers between devices, with_halo(): lax.ppermute(head, axis, [((i + 1) % count, i) for i in range(count)])  6.12 us
    unnamed x22, local copies, waits for them, and re-layouts  4.78 us
    dot_general x9, matrix products, body(): jnp.einsum('ijc,cd->ijd', padded[p:p + rows_dev, q:q + tile_cols], w_conv...  3.17 us
    dot_general x9, matrix products, body(): jnp.einsum('ijc,ijd->cd', padded[p:p + rows_dev, q:q + tile_cols], grad_p...  3.14 us
    dot_general x9, matrix products, body(): jnp.einsum('ijd,cd->ijc', padded_grad[2 - p:2 - p + rows_dev, 2 - q:2 - q...  3.11 us
  transfers between devices with their start and end apart: 4, of which 2 were waited for; matrix products, arithmetic and copies ran while one was open for 3% of the time, Pallas kernels for 0%

profile of v3, /device:TPU:0, one launch (start us, length us, event | category | flops | bytes accessed | tf_op | source)
XLA Modules:
  0.0 122.5 jit_solution(1031605722327220826)
XLA Ops:
  0.6 0.7 fusion.91.tile_ref.slot_ref
  1.3 0.7 fusion.89.rate_ref
  2.0 1.0 copy-done
  2.9 0.8 copy-done.1
  3.8 0.8 copy-done.3
  4.6 23.2 %shard_map.103 = f32[8,4,9,8,128]{4,3,2,1,0:T(8,128)S(1)} custom-call(s32[64]{0:T(128)S(1)} %fusion.91.tile_ref.slot_ref, f32[9]{0:T(128)S(1)} %fusion.89.rate_ref, bf16[64,2,256]{2,1,0:T(2,128)(2,1)S(1)} %copy-done.1, bf16[64,8,256]{2,1,0:T(8,128)(2,1)S(1)} %copy-done, s32[64,256]{1,0:T(8,128)S(1)} %copy-done.3), custom_call_target="tpu_custom_call" | custom-call | tf_op jit(solution)/shard_map/pallas_call | solution.py:349
  27.8 25.7 %shard_map.104 = f32[3,10,16,128]{3,2,1,0:T(8,128)S(1)} custom-call(f32[2,16,72,128]{3,2,1,0:T(8,128)S(1)} %bitcast.159), custom_call_target="tpu_custom_call" | custom-call | tf_op jit(solution)/shard_map/pallas_call | solution.py:360
  53.9 0.2 copy.14
  54.1 0.2 copy.13
  54.3 1.6 %convolution_convert_fusion = bf16[10,130,256]{2,1,0:T(8,128)(2,1)S(1)} fusion(f32[10,9,1]{2,1,0:T(8,128)S(1)} %copy.14, f32[10,9,128]{2,1,0:T(8,128)S(1)} %slice_bitcast_fusion, f32[10,9,1]{2,1,0:T(8,128)S(1)} %copy.13, f32[9,256]{1,0:T(8,128)S(1)} %copy-done.9), kind=kOutput, calls=%fused_computation.18 | convolution fusion | flops 36298600 | bytes 721616 | tf_op jit(solution)/shard_map/ikj,kc->ijc/dot_general | solution.py:384
  55.9 0.3 fusion.41
  56.2 0.3 convolution_add_fusion.16
  56.5 0.3 convolution_add_fusion.15
  56.8 0.3 convolution_add_fusion.14
  57.1 0.3 convolution_add_fusion.13
  57.5 0.3 convolution_add_fusion.12
  57.8 0.3 convolution_add_fusion.11
  58.1 0.3 convolution_add_fusion.10
  58.4 0.7 copy-done.7
  59.1 0.7 fusion.10
  59.9 5.6 %collective-permute-start.1 = (bf16[1,128,256]{2,1,0:T(8,128)(2,1)S(1)}, bf16[1,128,256]{2,1,0:T(8,128)(2,1)S(1)}, u32[]{:S(2)}, u32[]{:S(2)}) collective-permute-start(bf16[1,128,256]{2,1,0:T(8,128)(2,1)S(1)} %get-tuple-element.12), channel_id=1, source_target_pairs={{1,0},{2,1},{3,2},{8,3},{9,8},{10,9},{11,10},{16,11},{17,16},{18,1... | collective-permute-start | bytes 196616 | tf_op jit(solution)/shard_map/ppermute | solution.py:18
  65.5 0.3 fusion.8
  65.9 0.3 fusion.7
  66.2 0.4 fusion.6
  66.6 0.3 fusion.5
  67.0 0.4 fusion.4
  67.3 0.4 fusion.3
  67.7 0.4 fusion.2
  68.0 0.4 fusion.1
  68.4 0.4 fusion
  68.9 0.5 collective-permute-start.3
  69.4 0.7 collective-permute-done.2
  70.3 0.4 maximum_multiply_fusion
  70.7 0.3 convolution_add_fusion.8
  71.0 0.3 convolution_add_fusion.7
  71.4 0.3 convolution_add_fusion.6
  71.7 0.4 convolution_add_fusion.5
  72.1 0.4 convolution_add_fusion.4
  72.5 0.3 convolution_add_fusion.3
  72.8 0.4 convolution_add_fusion.2
  73.1 0.4 convolution_add_fusion.1
  73.5 0.3 convolution_add_fusion
  73.9 0.5 convolution_bitcast_fusion.9
  74.4 1.0 fusion.9
  75.4 44.0 %shard_map.105 = (f32[64,8,256]{2,1,0:T(8,128)S(1)}, f32[16,256]{1,0:T(8,128)S(1)}, bf16[2,4,4,72,256]{4,3,2,1,0:T(8,128)(2,1)S(1)}) custom-call(s32[64]{0:T(128)S(1)} %fusion.91.tile_ref.slot_ref, f32[9]{0:T(128)S(1)} %fusion.89.rate_ref, bf16[64,2,256]{2,1,0:T(2,128)(2,1)S(1)} %copy-done.2, s32[64,256]{1,0:T(8,128)S(1)} %copy-done.4, ...), custom_call_target="tpu_custom_call" | custom-call | flops 4000000000 | bytes 8000000 | tf_op jit(solution)/shard_map/pallas_call | solution.py:427
  119.5 1.6 %convert.1 = f32[3,3,256,256]{3,2,1,0:T(8,128)} convert(bf16[3,3,256,256]{3,2,1,0:T(8,128)(2,1)S(1)} %bitcast.160) | non-fusion elementwise | flops 589824 | bytes 3538944 | tf_op jit(solution)/shard_map/reshape | solution.py:468
  121.1 0.6 copy.46
  121.7 0.8 copy.47
  (30 shorter events, 0.8 us)
Async XLA Ops:
  2.0 1.0 copy-start
  2.9 0.8 copy-start.1
  3.8 0.8 copy-start.3
  27.8 26.5 %copy-start.9 = (f32[9,256]{1,0:T(8,128)S(1)}, f32[9,256]{1,0:T(8,128)}, u32[]{:S(2)}) copy-start(f32[9,256]{1,0:T(8,128)} %param.13) | copy-start | bytes 27652
  27.8 28.0 %copy-start.5 = (bf16[3,3,256,256]{3,2,1,0:T(8,128)(2,1)S(1)}, bf16[3,3,256,256]{3,2,1,0:T(8,128)(2,1)}, u32[]{:S(2)}) copy-start(bf16[3,3,256,256]{3,2,1,0:T(8,128)(2,1)} %param.14) | copy-start | bytes 3538948
  58.1 1.0 copy-start.7
  59.9 8.9 %collective-permute-start = (bf16[1,128,256]{2,1,0:T(8,128)(2,1)S(1)}, bf16[1,128,256]{2,1,0:T(8,128)(2,1)S(1)}, u32[]{:S(2)}, u32[]{:S(2)}) collective-permute-start(bf16[1,128,256]{2,1,0:T(8,128)(2,1)S(1)} %get-tuple-element.11), channel_id=1, source_target_pairs={{0,1},{1,2},{2,3},{3,8},{8,9},{9,10},{10,11},{11,16},{16,17},{17,1... | collective-permute-start | bytes 196616 | tf_op jit(solution)/shard_map/ppermute | solution.py:16
  59.9 8.9 %collective-permute-start.1 = (bf16[1,128,256]{2,1,0:T(8,128)(2,1)S(1)}, bf16[1,128,256]{2,1,0:T(8,128)(2,1)S(1)}, u32[]{:S(2)}, u32[]{:S(2)}) collective-permute-start(bf16[1,128,256]{2,1,0:T(8,128)(2,1)S(1)} %get-tuple-element.12), channel_id=1, source_target_pairs={{1,0},{2,1},{3,2},{8,3},{9,8},{10,9},{11,10},{16,11},{17,16},{18,1... | collective-permute-start | bytes 196616 | tf_op jit(solution)/shard_map/ppermute | solution.py:18
  68.8 1.9 %copy-start.6 = (bf16[3,3,256,256]{3,2,1,0:T(8,128)(2,1)S(1)}, bf16[3,3,256,256]{3,2,1,0:T(8,128)(2,1)}, u32[]{:S(2)}) copy-start(bf16[3,3,256,256]{3,2,1,0:T(8,128)(2,1)} %param.14) | copy-start | bytes 3538948
  68.8 1.9 %copy-start.8 = (bf16[8,128,256]{2,1,0:T(8,128)(2,1)S(1)}, bf16[8,128,256]{2,1,0:T(8,128)(2,1)}, u32[]{:S(2)}) copy-start(bf16[8,128,256]{2,1,0:T(8,128)(2,1)} %param.15) | copy-start | bytes 1572868
  68.8 1.2 %collective-permute-start.2 = (bf16[10,1,256]{2,1,0:T(2,128)(2,1)S(1)}, bf16[10,1,256]{2,1,0:T(2,128)(2,1)S(1)}, u32[]{:S(2)}, u32[]{:S(2)}) collective-permute-start(bf16[10,1,256]{2,1,0:T(2,128)(2,1)S(1)} %get-tuple-element.9), channel_id=1, source_target_pairs={{0,4},{4,0},{1,5},{5,1},{2,6},{6,2},{3,7},{7,3},{8,12},{12,8},{9,1... | collective-permute-start | bytes 15368 | tf_op jit(solution)/shard_map/ppermute | solution.py:16
  68.9 1.3 %collective-permute-start.3 = (bf16[10,1,256]{2,1,0:T(2,128)(2,1)S(1)}, bf16[10,1,256]{2,1,0:T(2,128)(2,1)S(1)}, u32[]{:S(2)}, u32[]{:S(2)}) collective-permute-start(bf16[10,1,256]{2,1,0:T(2,128)(2,1)S(1)} %get-tuple-element.10), channel_id=1, source_target_pairs={{4,0},{0,4},{5,1},{1,5},{6,2},{2,6},{7,3},{3,7},{12,8},{8,12},{13,... | collective-permute-start | bytes 15368 | tf_op jit(solution)/shard_map/ppermute | solution.py:18
  73.8 1.6 %copy-start.2 = (bf16[64,2,256]{2,1,0:T(2,128)(2,1)S(1)}, bf16[64,2,256]{2,1,0:T(2,128)(2,1)}, u32[]{:S(2)}) copy-start(bf16[64,2,256]{2,1,0:T(2,128)(2,1)} %coords_ref.3) | copy-start | bytes 196612
  73.9 1.6 %copy-start.4 = (s32[64,256]{1,0:T(8,128)S(1)}, s32[64,256]{1,0:T(8,128)}, u32[]{:S(2)}) copy-start(s32[64,256]{1,0:T(8,128)} %live_ref.3) | copy-start | bytes 196612

commit v4 on v3

--- a/solution.py
+++ b/solution.py
@@ -33,6 +33,17 @@
     return -1.4426950408889634 / (2.0 * lengthscale * lengthscale)
 
 
+def each_block(first, last, one):
+    together = 4 if first % 4 == 0 and last % 4 == 0 else 1
+
+    def several(m, carry):
+        for i in range(together):
+            carry = one(m * together + i, carry)
+        return carry
+
+    lax.fori_loop(first // together, last // together, several, 0)
+
+
 def gather_kernel(tile_ref, rate_ref, coords_ref, values_ref, live_ref, out_ref, total):
     variables = values_ref.shape[1]
     tile_rows, tile_cols = total.shape[2:]
@@ -55,7 +66,7 @@
             )
         return carry
 
-    lax.fori_loop(0, coords_ref.shape[0], one, 0)
+    each_block(0, coords_ref.shape[0], one)
 
     def flush(t, carry):
         for o in range(tile_rows // rows_dev):
@@ -275,7 +286,7 @@
         return carry
 
     def some(first, last):
-        lax.fori_loop(first * blocks // 64, last * blocks // 64, one, 0)
+        each_block(first * blocks // 64, last * blocks // 64, one)
 
     some(0, 8)
     wait_all(reduce2)
@@ -297,15 +308,15 @@
     whole[lon, lat, obs] = value.astype(jnp.bfloat16)
     mine1 = whole.at[lon, lat, obs]
     spread1 = start_copies("obs", lambda peer: mine1, mine1, sems.at[9])
-    some(24, 34)
+    some(24, 36)
     wait_all(spread1)
     mine2 = whole.at[lon, lat]
     spread2 = start_copies("lat", lambda peer: mine2, mine2, sems.at[10])
-    some(34, 54)
+    some(36, 52)
     wait_all(spread2)
     mine3 = whole.at[lon]
     spread3 = start_copies("lon", lambda peer: mine3, mine3, sems.at[11])
-    some(54, 64)
+    some(52, 64)
     wait_all(spread3)
 
     def give(i, carry):

time: 123 us -> 116 us (0.943)
  Pallas kernels: 92.9 us -> 86.3 us
    pallas_call x1, Pallas kernels: 23.2 us -> 16.7 us  [body(): pl.pallas_call(gather_kernel, out_shape=jax.ShapeDtypeStruct((tiles, obs_...]
where the time goes in v4:
time: 116 us
  Pallas kernels  86.3 us (74%)
  matrix products  12.5 us (11%)
  starting transfers between devices  6.25 us (5%)
  local copies, waits for them, and re-layouts  5.56 us (5%)
  other arithmetic  3.38 us (3%)
    pallas_call x1, Pallas kernels, body(): pl.pallas_call(value_kernel, out_shape=(jax.ShapeDtypeStruct((blocks, var...  43.9 us
    pallas_call x1, Pallas kernels, body(): pl.pallas_call(reduce_kernel, out_shape=jax.ShapeDtypeStruct((3, rows_dev...  25.7 us
    pallas_call x1, Pallas kernels, body(): pl.pallas_call(gather_kernel, out_shape=jax.ShapeDtypeStruct((tiles, obs_...  16.7 us
    ppermute x2, starting transfers between devices, with_halo(): lax.ppermute(head, axis, [((i + 1) % count, i) for i in range(count)])  6.12 us
    unnamed x22, local copies, waits for them, and re-layouts  4.78 us
    dot_general x9, matrix products, body(): jnp.einsum('ijc,cd->ijd', padded[p:p + rows_dev, q:q + tile_cols], w_conv...  3.17 us
    dot_general x9, matrix products, body(): jnp.einsum('ijc,ijd->cd', padded[p:p + rows_dev, q:q + tile_cols], grad_p...  3.14 us
    dot_general x9, matrix products, body(): jnp.einsum('ijd,cd->ijc', padded_grad[2 - p:2 - p + rows_dev, 2 - q:2 - q...  3.11 us
  transfers between devices with their start and end apart: 4, of which 2 were waited for; matrix products, arithmetic and copies ran while one was open for 3% of the time, Pallas kernels for 0%

profile of v4, /device:TPU:0, one launch (start us, length us, event | category | flops | bytes accessed | tf_op | source)
XLA Modules:
  0.0 115.9 jit_solution(11943662149511411816)
XLA Ops:
  0.6 0.7 fusion.91.tile_ref.slot_ref
  1.3 0.7 fusion.89.rate_ref
  2.0 1.0 copy-done
  2.9 0.8 copy-done.1
  3.8 0.8 copy-done.3
  4.6 16.7 %shard_map.103 = f32[8,4,9,8,128]{4,3,2,1,0:T(8,128)S(1)} custom-call(s32[64]{0:T(128)S(1)} %fusion.91.tile_ref.slot_ref, f32[9]{0:T(128)S(1)} %fusion.89.rate_ref, bf16[64,2,256]{2,1,0:T(2,128)(2,1)S(1)} %copy-done.1, bf16[64,8,256]{2,1,0:T(8,128)(2,1)S(1)} %copy-done, s32[64,256]{1,0:T(8,128)S(1)} %copy-done.3), custom_call_target="tpu_custom_call" | custom-call | tf_op jit(solution)/shard_map/pallas_call | solution.py:360
  21.3 25.7 %shard_map.104 = f32[3,10,16,128]{3,2,1,0:T(8,128)S(1)} custom-call(f32[2,16,72,128]{3,2,1,0:T(8,128)S(1)} %bitcast.159), custom_call_target="tpu_custom_call" | custom-call | tf_op jit(solution)/shard_map/pallas_call | solution.py:371
  47.4 0.2 copy.14
  47.6 0.2 copy.13
  47.8 1.6 %convolution_convert_fusion = bf16[10,130,256]{2,1,0:T(8,128)(2,1)S(1)} fusion(f32[10,9,1]{2,1,0:T(8,128)S(1)} %copy.14, f32[10,9,128]{2,1,0:T(8,128)S(1)} %slice_bitcast_fusion, f32[10,9,1]{2,1,0:T(8,128)S(1)} %copy.13, f32[9,256]{1,0:T(8,128)S(1)} %copy-done.9), kind=kOutput, calls=%fused_computation.18 | convolution fusion | flops 36298600 | bytes 721616 | tf_op jit(solution)/shard_map/ikj,kc->ijc/dot_general | solution.py:395
  49.4 0.3 fusion.41
  49.7 0.3 convolution_add_fusion.16
  50.0 0.3 convolution_add_fusion.15
  50.3 0.3 convolution_add_fusion.14
  50.6 0.3 convolution_add_fusion.13
  50.9 0.3 convolution_add_fusion.12
  51.3 0.3 convolution_add_fusion.11
  51.6 0.3 convolution_add_fusion.10
  51.9 0.7 copy-done.7
  52.6 0.7 fusion.10
  53.4 5.6 %collective-permute-start.1 = (bf16[1,128,256]{2,1,0:T(8,128)(2,1)S(1)}, bf16[1,128,256]{2,1,0:T(8,128)(2,1)S(1)}, u32[]{:S(2)}, u32[]{:S(2)}) collective-permute-start(bf16[1,128,256]{2,1,0:T(8,128)(2,1)S(1)} %get-tuple-element.12), channel_id=1, source_target_pairs={{1,0},{2,1},{3,2},{8,3},{9,8},{10,9},{11,10},{16,11},{17,16},{18,1... | collective-permute-start | bytes 196616 | tf_op jit(solution)/shard_map/ppermute | solution.py:18
  59.0 0.3 fusion.8
  59.4 0.3 fusion.7
  59.7 0.4 fusion.6
  60.1 0.3 fusion.5
  60.4 0.4 fusion.4
  60.8 0.4 fusion.3
  61.1 0.4 fusion.2
  61.5 0.4 fusion.1
  61.9 0.4 fusion
  62.4 0.5 collective-permute-start.3
  62.9 0.7 collective-permute-done.2
  63.7 0.4 maximum_multiply_fusion
  64.1 0.3 convolution_add_fusion.8
  64.5 0.3 convolution_add_fusion.7
  64.9 0.3 convolution_add_fusion.6
  65.2 0.4 convolution_add_fusion.5
  65.6 0.4 convolution_add_fusion.4
  65.9 0.3 convolution_add_fusion.3
  66.3 0.4 convolution_add_fusion.2
  66.6 0.4 convolution_add_fusion.1
  67.0 0.3 convolution_add_fusion
  67.3 0.5 convolution_bitcast_fusion.9
  67.9 1.0 fusion.9
  68.9 43.9 %shard_map.105 = (f32[64,8,256]{2,1,0:T(8,128)S(1)}, f32[16,256]{1,0:T(8,128)S(1)}, bf16[2,4,4,72,256]{4,3,2,1,0:T(8,128)(2,1)S(1)}) custom-call(s32[64]{0:T(128)S(1)} %fusion.91.tile_ref.slot_ref, f32[9]{0:T(128)S(1)} %fusion.89.rate_ref, bf16[64,2,256]{2,1,0:T(2,128)(2,1)S(1)} %copy-done.2, s32[64,256]{1,0:T(8,128)S(1)} %copy-done.4, ...), custom_call_target="tpu_custom_call" | custom-call | flops 4000000000 | bytes 8000000 | tf_op jit(solution)/shard_map/pallas_call | solution.py:438
  112.8 1.6 %convert.1 = f32[3,3,256,256]{3,2,1,0:T(8,128)} convert(bf16[3,3,256,256]{3,2,1,0:T(8,128)(2,1)S(1)} %bitcast.160) | non-fusion elementwise | flops 589824 | bytes 3538944 | tf_op jit(solution)/shard_map/reshape | solution.py:479
  114.5 0.6 copy.46
  115.1 0.8 copy.47
  (30 shorter events, 0.8 us)
Async XLA Ops:
  2.0 1.0 copy-start
  2.9 0.8 copy-start.1
  3.8 0.8 copy-start.3
  21.3 26.5 %copy-start.9 = (f32[9,256]{1,0:T(8,128)S(1)}, f32[9,256]{1,0:T(8,128)}, u32[]{:S(2)}) copy-start(f32[9,256]{1,0:T(8,128)} %param.13) | copy-start | bytes 27652
  21.3 28.1 %copy-start.5 = (bf16[3,3,256,256]{3,2,1,0:T(8,128)(2,1)S(1)}, bf16[3,3,256,256]{3,2,1,0:T(8,128)(2,1)}, u32[]{:S(2)}) copy-start(bf16[3,3,256,256]{3,2,1,0:T(8,128)(2,1)} %param.14) | copy-start | bytes 3538948
  51.6 1.0 copy-start.7
  53.3 8.9 %collective-permute-start = (bf16[1,128,256]{2,1,0:T(8,128)(2,1)S(1)}, bf16[1,128,256]{2,1,0:T(8,128)(2,1)S(1)}, u32[]{:S(2)}, u32[]{:S(2)}) collective-permute-start(bf16[1,128,256]{2,1,0:T(8,128)(2,1)S(1)} %get-tuple-element.11), channel_id=1, source_target_pairs={{0,1},{1,2},{2,3},{3,8},{8,9},{9,10},{10,11},{11,16},{16,17},{17,1... | collective-permute-start | bytes 196616 | tf_op jit(solution)/shard_map/ppermute | solution.py:16
  53.4 8.9 %collective-permute-start.1 = (bf16[1,128,256]{2,1,0:T(8,128)(2,1)S(1)}, bf16[1,128,256]{2,1,0:T(8,128)(2,1)S(1)}, u32[]{:S(2)}, u32[]{:S(2)}) collective-permute-start(bf16[1,128,256]{2,1,0:T(8,128)(2,1)S(1)} %get-tuple-element.12), channel_id=1, source_target_pairs={{1,0},{2,1},{3,2},{8,3},{9,8},{10,9},{11,10},{16,11},{17,16},{18,1... | collective-permute-start | bytes 196616 | tf_op jit(solution)/shard_map/ppermute | solution.py:18
  62.2 1.9 %copy-start.6 = (bf16[3,3,256,256]{3,2,1,0:T(8,128)(2,1)S(1)}, bf16[3,3,256,256]{3,2,1,0:T(8,128)(2,1)}, u32[]{:S(2)}) copy-start(bf16[3,3,256,256]{3,2,1,0:T(8,128)(2,1)} %param.14) | copy-start | bytes 3538948
  62.3 1.9 %copy-start.8 = (bf16[8,128,256]{2,1,0:T(8,128)(2,1)S(1)}, bf16[8,128,256]{2,1,0:T(8,128)(2,1)}, u32[]{:S(2)}) copy-start(bf16[8,128,256]{2,1,0:T(8,128)(2,1)} %param.15) | copy-start | bytes 1572868
  62.3 1.2 %collective-permute-start.2 = (bf16[10,1,256]{2,1,0:T(2,128)(2,1)S(1)}, bf16[10,1,256]{2,1,0:T(2,128)(2,1)S(1)}, u32[]{:S(2)}, u32[]{:S(2)}) collective-permute-start(bf16[10,1,256]{2,1,0:T(2,128)(2,1)S(1)} %get-tuple-element.9), channel_id=1, source_target_pairs={{0,4},{4,0},{1,5},{5,1},{2,6},{6,2},{3,7},{7,3},{8,12},{12,8},{9,1... | collective-permute-start | bytes 15368 | tf_op jit(solution)/shard_map/ppermute | solution.py:16
  62.4 1.3 %collective-permute-start.3 = (bf16[10,1,256]{2,1,0:T(2,128)(2,1)S(1)}, bf16[10,1,256]{2,1,0:T(2,128)(2,1)S(1)}, u32[]{:S(2)}, u32[]{:S(2)}) collective-permute-start(bf16[10,1,256]{2,1,0:T(2,128)(2,1)S(1)} %get-tuple-element.10), channel_id=1, source_target_pairs={{4,0},{0,4},{5,1},{1,5},{6,2},{2,6},{7,3},{3,7},{12,8},{8,12},{13,... | collective-permute-start | bytes 15368 | tf_op jit(solution)/shard_map/ppermute | solution.py:18
  67.3 1.6 %copy-start.2 = (bf16[64,2,256]{2,1,0:T(2,128)(2,1)S(1)}, bf16[64,2,256]{2,1,0:T(2,128)(2,1)}, u32[]{:S(2)}) copy-start(bf16[64,2,256]{2,1,0:T(2,128)(2,1)} %coords_ref.3) | copy-start | bytes 196612
  67.3 1.6 %copy-start.4 = (s32[64,256]{1,0:T(8,128)S(1)}, s32[64,256]{1,0:T(8,128)}, u32[]{:S(2)}) copy-start(s32[64,256]{1,0:T(8,128)} %live_ref.3) | copy-start | bytes 196612
